TPU v7x, 256 devices: a whole 4x4x8 slice. The times are simulated.
256 devices in a mesh: grp: 16 (over z_hi, y, core), seq: 4 (over z_lo), head: 4 (over x).
Axes of the slice: x: 4, y: 4, z: 8 (z_hi: 2, z_lo: 4; z = z_hi * 4 + z_lo), core: 2. Of those that a mesh axis runs over, the one named last changes fastest.
Arguments:
- t_query: bfloat16 [16, 1024, 2048], P('grp', 'seq', 'head'), may hold values from -8 to 8
- t_key: bfloat16 [16, 1024, 2048], P('grp', 'seq', 'head'), may hold values from -4 to 4
- t_value: bfloat16 [16, 1024, 2048], P('grp', 'seq', 'head'), may hold values from -6 to 6
- out_proj: bfloat16 [2048, 4096], P('head', 'seq'), may hold values from -0.125 to 0.125
- depth_in: bfloat16 [2, 4096, 1024], P(None, 'seq'), may hold values from -0.09375 to 0.09375
- prev_embed: bfloat16 [16, 4, 256, 2, 1024], P('grp', 'head', 'seq'), may hold values from -3 to 3
- cotangent: bfloat16 [16, 4, 256, 2, 1024], P('grp', 'head', 'seq'), may hold values from -0.59765625 to 0.59765625
Outputs:
- d_query: float32 [16, 1024, 2048], P('grp', 'seq', 'head')
- d_key: float32 [16, 1024, 2048], P('grp', 'seq', 'head')
- d_value: float32 [16, 1024, 2048], P('grp', 'seq', 'head')
- d_out_proj: float32 [2048, 4096], P('head', 'seq')
- d_depth_in: float32 [2, 4096, 1024], P(None, ('seq', 'head'), 'grp')
All inputs are finite; a program needn't handle non-finite values.
Results may differ from a plain program's by a relative error of at most 0.023.
Values may be sent and summed in bfloat16 or wider, within the bound.
A program may use at most 128 MiB of HBM per device.

v0:
```python
import jax
import jax.numpy as jnp
from jax import lax
from jax.sharding import PartitionSpec as P

HD = 128


def shards(t_query, t_key, t_value, out_proj, depth_in, prev_embed, cotangent):
    tok_rows = t_query.shape[1]
    feat_width = t_query.shape[2]
    head_count = feat_width // HD
    score_scale = HD ** (-0.5)
    seq_length = tok_rows * lax.axis_size("seq")
    all_keys, all_values = (
        lax.all_gather(t_key[0], "seq", axis=0, tiled=True),
        lax.all_gather(t_value[0], "seq", axis=0, tiled=True),
    )
    query_heads = t_query[0].reshape(tok_rows, head_count, HD)
    key_heads = all_keys.reshape(seq_length, head_count, HD)
    value_heads = all_values.reshape(seq_length, head_count, HD)
    scores = (
        jnp.einsum("qhd,khd->hqk", query_heads, key_heads, preferred_element_type=jnp.float32)
        * score_scale
    )
    query_pos = lax.axis_index("seq") * tok_rows + lax.iota(jnp.int32, tok_rows)
    key_pos = lax.iota(jnp.int32, seq_length)
    causal = query_pos[:, None] >= key_pos[None, :]
    scores = jnp.where(causal, scores, -1e30)
    row_max = jnp.max(scores, axis=-1, keepdims=True)
    expo_terms = jnp.where(causal, jnp.exp(scores - row_max), 0.0)
    row_total = jnp.sum(expo_terms, axis=-1)
    mixed_heads = jnp.einsum(
        "hqk,khd->qhd",
        expo_terms.astype(jnp.bfloat16),
        value_heads,
        preferred_element_type=jnp.float32,
    )
    mixed_heads = mixed_heads / jnp.transpose(row_total)[:, :, None]
    attended = mixed_heads.reshape(tok_rows, feat_width).astype(jnp.bfloat16)
    probability = expo_terms / row_total[:, :, None]
    all_heads = lax.all_gather(attended, "seq", axis=0, tiled=True)
    head_rows = all_heads
    context = lax.psum_scatter(
        jnp.dot(head_rows, out_proj, preferred_element_type=jnp.float32),
        "head",
        scatter_dimension=0,
        tiled=True,
    ).astype(jnp.bfloat16)
    depth_x = lax.psum_scatter(
        jnp.einsum("fd,kdc->fkc", context, depth_in, preferred_element_type=jnp.float32),
        "seq",
        scatter_dimension=0,
        tiled=True,
    )
    depth_x = depth_x + prev_embed[0, 0].astype(jnp.float32)
    inverse = lax.rsqrt(jnp.mean(depth_x * depth_x, axis=-1, keepdims=True) + 1e-05)
    normed = depth_x * inverse
    grad_out = cotangent[0, 0].astype(jnp.float32)
    grad_x = inverse * (grad_out - normed * jnp.mean(grad_out * normed, axis=-1, keepdims=True))
    grad_x = grad_x.astype(jnp.bfloat16)
    grad_block = lax.all_gather(grad_x, "seq", axis=0, tiled=True)
    grad_context = jnp.einsum(
        "fkc,kdc->fd", grad_block, depth_in, preferred_element_type=jnp.float32
    ).astype(jnp.bfloat16)
    win_terms = jnp.einsum("fd,fkc->kdc", context, grad_block, preferred_element_type=jnp.float32)
    section_one = lax.psum_scatter(
        win_terms.astype(jnp.bfloat16), "grp", scatter_dimension=2, tiled=True
    )
    grad_depth = lax.psum_scatter(section_one, "head", scatter_dimension=1, tiled=True).astype(
        jnp.float32
    )
    shard_rows = lax.all_gather(grad_context, "head", axis=0, tiled=True)
    head_rows = all_heads
    wo_terms = jnp.einsum("fw,fd->wd", head_rows, shard_rows, preferred_element_type=jnp.float32)
    out_rows = jnp.einsum("fd,wd->fw", shard_rows, out_proj, preferred_element_type=jnp.float32)
    out_terms = out_rows
    wo_terms, out_terms = (wo_terms, out_terms)
    grad_proj = lax.psum(wo_terms.astype(jnp.bfloat16), "grp").astype(jnp.float32)
    grad_attended = lax.psum_scatter(out_terms, "seq", scatter_dimension=0, tiled=True).astype(
        jnp.bfloat16
    )
    grad_heads = grad_attended.reshape(tok_rows, head_count, HD)
    grad_probs = jnp.einsum(
        "qhd,khd->hqk", grad_heads, value_heads, preferred_element_type=jnp.float32
    )
    attended_heads = attended.reshape(tok_rows, head_count, HD).astype(jnp.float32)
    delta_rows = jnp.transpose(jnp.sum(grad_heads.astype(jnp.float32) * attended_heads, axis=-1))
    grad_scores = (probability * (grad_probs - delta_rows[:, :, None])).astype(jnp.bfloat16)
    grad_query = (
        jnp.einsum("hqk,khd->qhd", grad_scores, key_heads, preferred_element_type=jnp.float32)
        * score_scale
    )
    key_terms = (
        jnp.einsum("hqk,qhd->khd", grad_scores, query_heads, preferred_element_type=jnp.float32)
        * score_scale
    )
    value_terms = jnp.einsum(
        "hqk,qhd->khd",
        probability.astype(jnp.bfloat16),
        grad_heads,
        preferred_element_type=jnp.float32,
    )
    grad_key, grad_value = (
        lax.psum_scatter(
            key_terms.reshape(seq_length, feat_width).astype(jnp.bfloat16),
            "seq",
            scatter_dimension=0,
            tiled=True,
        ).astype(jnp.float32),
        lax.psum_scatter(
            value_terms.reshape(seq_length, feat_width).astype(jnp.bfloat16),
            "seq",
            scatter_dimension=0,
            tiled=True,
        ).astype(jnp.float32),
    )
    return (
        grad_query.reshape(1, tok_rows, feat_width),
        grad_key[None],
        grad_value[None],
        grad_proj,
        grad_depth,
    )


def solution(mesh):
    placed = (
        P("grp", "seq", "head"),
        P("grp", "seq", "head"),
        P("grp", "seq", "head"),
        P("head", "seq"),
        P(None, "seq", None),
        P("grp", "head", "seq", None, None),
        P("grp", "head", "seq", None, None),
    )
    return jax.shard_map(
        shards,
        mesh=mesh,
        in_specs=placed,
        out_specs=(
            P("grp", "seq", "head"),
            P("grp", "seq", "head"),
            P("grp", "seq", "head"),
            P("head", "seq"),
            P(None, ("seq", "head"), "grp"),
        ),
        check_vma=False,
    )
```

profile of v0, /device:TPU:1, one launch (start us, length us, event | category | flops | bytes accessed | tf_op | source)
XLA Modules:
  0.0 748.0 jit_solution(10570034432731632905)
XLA Ops:
  7.2 0.0 all-gather.14.cloned.1.call-start
  7.2 1.9 copy.24
  9.1 0.0 all-gather.14.cloned.1.call-update
  9.1 0.0 all-gather.16.cloned.1.call-start
  9.2 0.7 all-gather.16.cloned.1.call-update
  9.9 0.0 all-gather.8.cloned.1.call-start
  9.9 1.1 copy.40
  11.0 0.2 iota_compare_fusion
  11.3 39.4 %all-gather.14.cloned.1.call-done = bf16[1,1024,512]{1,2,0:T(8,128)(2,1)} async-done(((bf16[1,256,512]{1,2,0:T(8,128)(2,1)}), bf16[1,1024,512]{1,2,0:T(8,128)(2,1)}) %all-gather.14.cloned.1.call-update) | async-done | bytes 1048592 | tf_op jit(solution)/shard_map/all_gather | solution.py:16
  50.7 5.2 fusion.34
  55.9 27.6 %all-gather.16.cloned.1.call-done = bf16[1,1024,512]{2,1,0:T(8,128)(2,1)} async-done(((bf16[1,256,512]{2,1,0:T(8,128)(2,1)}), bf16[1,1024,512]{2,1,0:T(8,128)(2,1)}) %all-gather.16.cloned.1.call-update) | async-done | bytes 1048592 | tf_op jit(solution)/shard_map/all_gather | solution.py:17
  83.5 1.5 copy.27
  85.0 4.1 fusion.19
  89.1 0.0 all-gather.8.cloned.1.call-update
  89.2 0.0 reduce-scatter.8.cloned.1.call-start
  89.2 35.8 %all-gather.8.cloned.1.call-done = bf16[1024,512]{0,1:T(8,128)(2,1)} async-done(((bf16[256,512]{0,1:T(8,128)(2,1)}), bf16[1024,512]{0,1:T(8,128)(2,1)}) %all-gather.8.cloned.1.call-update) | async-done | bytes 1048592 | tf_op jit(solution)/shard_map/all_gather | solution.py:42
  125.0 4.5 fusion.35
  129.5 0.0 reduce-scatter.8.cloned.1.call-update
  129.6 0.0 reduce-scatter.10.cloned.1.call-start
  129.6 47.2 %reduce-scatter.8.cloned.1.call-done = f32[256,1024]{1,0:T(8,128)} async-done(((f32[1024,1024]{1,0:T(8,128)}), f32[256,1024]{1,0:T(8,128)}) %reduce-scatter.8.cloned.1.call-update) | async-done | bytes 1048592 | tf_op jit(solution)/shard_map/reduce_scatter | solution.py:44
  176.8 5.1 fusion.26
  181.9 0.0 reduce-scatter.10.cloned.1.call-update
  181.9 0.0 all-gather.10.cloned.1.call-start
  181.9 48.8 %reduce-scatter.10.cloned.1.call-done = f32[64,2,1024]{2,0,1:T(8,128)} async-done(((f32[256,2,1024]{2,0,1:T(8,128)}), f32[64,2,1024]{2,0,1:T(8,128)}) %reduce-scatter.10.cloned.1.call-update) | async-done | bytes 524304 | tf_op jit(solution)/shard_map/reduce_scatter | solution.py:50
  230.7 1.2 multiply_reduce_fusion.1
  231.9 1.3 fusion.22
  233.2 2.0 fusion.24
  235.3 0.0 all-gather.10.cloned.1.call-update
  235.3 0.0 all-gather.12.cloned.1.call-start
  235.4 33.1 %all-gather.10.cloned.1.call-done = bf16[256,2,1024]{2,0,1:T(8,128)(2,1)} async-done(((bf16[64,2,1024]{2,0,1:T(8,128)(2,1)}), bf16[256,2,1024]{2,0,1:T(8,128)(2,1)}) %all-gather.10.cloned.1.call-update) | async-done | bytes 1048592 | tf_op jit(solution)/shard_map/all_gather | solution.py:62
  268.4 4.7 fusion.12
  273.1 0.0 all-gather.12.cloned.1.call-update
  273.1 0.0 reduce-scatter.18.cloned.1.call-start
  273.2 3.3 convert_bitcast_fusion
  276.5 0.0 reduce-scatter.18.cloned.1.call-update
  276.5 0.0 reduce-scatter.12.cloned.1.call-start
  276.5 29.3 %all-gather.12.cloned.1.call-done = bf16[1024,1024]{1,0:T(8,128)(2,1)} async-done(((bf16[256,1024]{1,0:T(8,128)(2,1)}), bf16[1024,1024]{1,0:T(8,128)(2,1)}) %all-gather.12.cloned.1.call-update) | async-done | bytes 2097168 | tf_op jit(solution)/shard_map/all_gather | solution.py:73
  305.9 4.2 fusion.36
  310.1 0.0 reduce-scatter.12.cloned.1.call-update
  310.1 0.0 all-reduce.2.cloned.1.call-start
  310.2 3.9 convolution_convert_fusion
  314.1 0.0 reduce-scatter.20.cloned.1.call-start
  314.2 99.0 %reduce-scatter.18.cloned.1.call-done = bf16[2,1024,64]{1,2,0:T(8,128)(2,1)} async-done(((bf16[2,1024,1024]{1,2,0:T(8,128)(2,1)}), bf16[2,1024,64]{1,2,0:T(8,128)(2,1)}) %reduce-scatter.18.cloned.1.call-update) | async-done | bytes 262160 | tf_op jit(solution)/shard_map/reduce_scatter | solution.py:67
  413.2 0.2 reduce-scatter.14.cloned.1.call-start
  413.4 49.1 %reduce-scatter.12.cloned.1.call-done = f32[256,512]{1,0:T(8,128)} async-done(((f32[1024,512]{1,0:T(8,128)}), f32[256,512]{1,0:T(8,128)}) %reduce-scatter.12.cloned.1.call-update) | async-done | bytes 524304 | tf_op jit(solution)/shard_map/reduce_scatter | solution.py:80
  462.6 1.1 convert_element_type.91
  463.7 0.1 copy.30
  463.8 0.1 multiply_reduce_fusion
  463.9 3.4 multiply_convert_fusion
  467.3 1.5 multiply_convert_fusion.1
  468.8 2.3 copy.34
  471.1 0.0 reduce-scatter.16.cloned.1.call-start
  471.1 3.7 fusion.9
  474.9 2.3 copy.35
  477.2 167.2 %all-reduce.2.cloned.1.call-done = bf16[512,1024]{1,0:T(8,128)(2,1)} async-done(((bf16[512,1024]{1,0:T(8,128)(2,1)}), bf16[512,1024]{1,0:T(8,128)(2,1)}) %all-reduce.2.cloned.1.call-update) | async-done | bytes 1048592 | tf_op jit(solution)/shard_map/psum | solution.py:79
  644.4 2.8 convert_element_type.103
  647.2 21.7 %reduce-scatter.20.cloned.1.call-done = bf16[2,256,64]{1,2,0:T(8,128)(2,1)} async-done(((bf16[2,1024,64]{1,2,0:T(8,128)(2,1)}), bf16[2,256,64]{1,2,0:T(8,128)(2,1)}) %reduce-scatter.20.cloned.1.call-update) | async-done | bytes 65552 | tf_op jit(solution)/shard_map/reduce_scatter | solution.py:70
  668.9 1.5 convert_element_type.106
  670.4 2.9 convolution_multiply_fusion
  673.2 2.0 copy.36
  675.3 30.3 %reduce-scatter.14.cloned.1.call-done = bf16[256,512]{1,0:T(8,128)(2,1)} async-done(((bf16[1024,512]{1,0:T(8,128)(2,1)}), bf16[256,512]{1,0:T(8,128)(2,1)}) %reduce-scatter.14.cloned.1.call-update) | async-done | bytes 262160 | tf_op jit(solution)/shard_map/reduce_scatter | solution.py:105
  705.6 1.8 bitcast_convert_fusion.1
  707.4 32.3 %reduce-scatter.16.cloned.1.call-done = bf16[256,512]{1,0:T(8,128)(2,1)} async-done(((bf16[1024,512]{1,0:T(8,128)(2,1)}), bf16[256,512]{1,0:T(8,128)(2,1)}) %reduce-scatter.16.cloned.1.call-update) | async-done | bytes 262160 | tf_op jit(solution)/shard_map/reduce_scatter | solution.py:111
  739.6 1.8 bitcast_convert_fusion
  (27 shorter events, 0.1 us)
Async XLA Ops:
  7.2 117.9 %copy-start = (bf16[512,1024]{1,0:T(8,128)(2,1)S(1)}, bf16[512,1024]{1,0:T(8,128)(2,1)}, u32[]{:S(2)}) copy-start(bf16[512,1024]{1,0:T(8,128)(2,1)} %param.10) | copy-start | bytes 3145732
  7.2 43.5 %all-gather.14.cloned.1.call-start = ((), (), s32[]{:S(2)}) async-start(), calls=%async_computation.18 | async-start | bytes 1310720 | tf_op jit(solution)/shard_map/all_gather | solution.py:16
  9.1 74.4 %all-gather.16.cloned.1.call-start = ((), (), s32[]{:S(2)}) async-start(), calls=%async_computation.19 | async-start | bytes 1310720 | tf_op jit(solution)/shard_map/all_gather | solution.py:17
  9.9 115.1 %all-gather.8.cloned.1.call-start = ((), (), s32[]{:S(2)}) async-start(), calls=%async_computation.7 | async-start | bytes 1310720 | tf_op jit(solution)/shard_map/all_gather | solution.py:42
  11.0 44.9 %copy-start.8 = (bf16[1,256,512]{1,2,0:T(8,128)(2,1)}, bf16[1,256,512]{1,2,0:T(8,128)(2,1)S(1)}, u32[]{:S(2)}) copy-start(bf16[1,256,512]{1,2,0:T(8,128)(2,1)S(1)} %copy.40) | copy-start | bytes 786436
  85.0 44.5 %copy-start.3 = (bf16[1,1024,512]{1,2,0:T(8,128)(2,1)}, bf16[1,1024,512]{1,2,0:T(8,128)(2,1)S(1)}, u32[]{:S(2)}) copy-start(bf16[1,1024,512]{1,2,0:T(8,128)(2,1)S(1)} %copy.27) | copy-start | bytes 3145732
  89.2 87.6 %reduce-scatter.8.cloned.1.call-start = ((), (), s32[]{:S(2)}) async-start(), calls=%async_computation.8 | async-start | bytes 5242880 | tf_op jit(solution)/shard_map/reduce_scatter | solution.py:44
  129.5 101.2 %copy-start.5 = (bf16[1,1,64,2,1024]{4,3,2,1,0:T(2,128)(2,1)S(1)}, bf16[1,1,64,2,1024]{4,3,2,1,0:T(2,128)(2,1)}, u32[]{:S(2)}) copy-start(bf16[1,1,64,2,1024]{4,3,2,1,0:T(2,128)(2,1)} %param.12) | copy-start | bytes 786436
  129.5 102.4 %copy-start.7 = (bf16[1,1,64,2,1024]{4,3,2,1,0:T(2,128)(2,1)S(1)}, bf16[1,1,64,2,1024]{4,3,2,1,0:T(2,128)(2,1)}, u32[]{:S(2)}) copy-start(bf16[1,1,64,2,1024]{4,3,2,1,0:T(2,128)(2,1)} %param.13) | copy-start | bytes 786436
  129.6 101.2 %reduce-scatter.10.cloned.1.call-start = ((), (), s32[]{:S(2)}) async-start(), calls=%async_computation.9 | async-start | bytes 2621440 | tf_op jit(solution)/shard_map/reduce_scatter | solution.py:50
  181.9 86.6 %all-gather.10.cloned.1.call-start = ((), (), s32[]{:S(2)}) async-start(), calls=%async_computation.10 | async-start | bytes 1310720 | tf_op jit(solution)/shard_map/all_gather | solution.py:62
  235.3 37.9 %copy-start.1 = (f32[256,1024]{1,0:T(8,128)S(1)}, f32[256,1024]{1,0:T(8,128)}, u32[]{:S(2)}) copy-start(f32[256,1024]{1,0:T(8,128)} %reduce-scatter.8.cloned.1.call-done) | copy-start | bytes 3145732
  235.3 70.6 %all-gather.12.cloned.1.call-start = ((), (), s32[]{:S(2)}) async-start(), calls=%async_computation.11 | async-start | bytes 2621440 | tf_op jit(solution)/shard_map/all_gather | solution.py:73
  268.4 4.8 copy-start.2
  273.1 140.1 %reduce-scatter.18.cloned.1.call-start = ((), (), s32[]{:S(2)}) async-start(), calls=%async_computation.16 | async-start | bytes 4456448 | tf_op jit(solution)/shard_map/reduce_scatter | solution.py:67
  276.5 33.7 %copy-start.6 = (bf16[1024,512]{0,1:T(8,128)(2,1)S(1)}, bf16[1024,512]{0,1:T(8,128)(2,1)}, u32[]{:S(2)}) copy-start(bf16[1024,512]{0,1:T(8,128)(2,1)} %all-gather.8.cloned.1.call-done) | copy-start | bytes 3145732
  276.5 186.1 %reduce-scatter.12.cloned.1.call-start = ((), (), s32[]{:S(2)}) async-start(), calls=%async_computation.12 | async-start | bytes 2621440 | tf_op jit(solution)/shard_map/reduce_scatter | solution.py:80
  310.1 153.7 %copy-start.4 = (bf16[256,4,128]{0,2,1:T(8,128)(2,1)S(1)}, bf16[256,4,128]{0,2,1:T(8,128)(2,1)}, u32[]{:S(2)}) copy-start(bf16[256,4,128]{0,2,1:T(8,128)(2,1)} %fusion.19) | copy-start | bytes 786436
  310.1 334.3 %all-reduce.2.cloned.1.call-start = ((), (), s32[]{:S(2)}) async-start(), calls=%async_computation.15 | async-start | bytes 2097152 | tf_op jit(solution)/shard_map/psum | solution.py:79
  314.1 354.7 %reduce-scatter.20.cloned.1.call-start = ((), (), s32[]{:S(2)}) async-start(), calls=%async_computation.17 | async-start | bytes 327680 | tf_op jit(solution)/shard_map/reduce_scatter | solution.py:70
  413.2 292.3 %reduce-scatter.14.cloned.1.call-start = ((), (), s32[]{:S(2)}) async-start(), calls=%async_computation.13 | async-start | bytes 1310720 | tf_op jit(solution)/shard_map/reduce_scatter | solution.py:105
  463.9 3.4 copy-start.9
  471.1 268.6 %reduce-scatter.16.cloned.1.call-start = ((), (), s32[]{:S(2)}) async-start(), calls=%async_computation.14 | async-start | bytes 1310720 | tf_op jit(solution)/shard_map/reduce_scatter | solution.py:111
Sparse Core Ops, SparseCore 0:
  10.4 40.2 all-gather.13
  52.5 30.9 all-gather.15
  89.3 35.6 all-gather.7
  129.6 47.0 reduce-scatter.7
  182.0 48.6 reduce-scatter.9
  235.4 32.9 all-gather.9
  273.3 32.5 all-gather.11
  310.2 102.9 reduce-scatter.17
  416.5 46.0 reduce-scatter.11
  465.1 179.2 all-reduce.1
  647.1 21.7 reduce-scatter.19
  671.3 34.2 reduce-scatter.13
  708.3 31.3 reduce-scatter.15
where the time goes:
time: 749 us; the launch traced here: 748 us
  waiting for transfers between devices  662 us (88%)
  matrix products  46.3 us (6%)
  between operations  14.1 us (2%)
  other arithmetic  13.8 us (2%)
  local copies, waits for them, and re-layouts  11.2 us (1%)
    psum x1, waiting for transfers between devices, shards(): lax.psum(wo_terms.astype(jnp.bfloat16), 'grp').astype(jnp.float32)  167 us
    reduce_scatter x1, waiting for transfers between devices, shards(): lax.psum_scatter(win_terms.astype(jnp.bfloat16), 'grp', scatter_dimension...  99 us
    reduce_scatter x1, waiting for transfers between devices, shards(): lax.psum_scatter(out_terms, 'seq', scatter_dimension=0, tiled=True)  49.1 us
    reduce_scatter x1, waiting for transfers between devices, shards(): lax.psum_scatter(jnp.einsum('fd,kdc->fkc', context, depth_in, preferred_e...  48.8 us
    reduce_scatter x1, waiting for transfers between devices, shards(): lax.psum_scatter(jnp.dot(head_rows, out_proj, preferred_element_type=jnp....  47.2 us
    all_gather x1, waiting for transfers between devices, shards(): lax.all_gather(t_key[0], 'seq', axis=0, tiled=True)  39.4 us
    all_gather x1, waiting for transfers between devices, shards(): all_heads = lax.all_gather(attended, 'seq', axis=0, tiled=True)  35.8 us
    all_gather x1, waiting for transfers between devices, shards(): grad_block = lax.all_gather(grad_x, 'seq', axis=0, tiled=True)  33.1 us
  transfers between devices with their start and end apart: 13, of which 13 were waited for; matrix products, arithmetic and copies ran while one was open for 6% of the time, Pallas kernels for 0%

commit v1 on v0

v1 whole, which is shorter than its diff:
```python
import jax
import jax.numpy as jnp
from jax import lax
from jax.experimental import pallas as pl
from jax.experimental.pallas import tpu as pltpu
from jax.sharding import PartitionSpec as P

MESH = pl.DeviceIdType.MESH
HD = 128
BF = jnp.bfloat16
F32 = jnp.float32
SCALE = HD ** (-0.5)
LOG2E = 1.4426950408889634


def nt(a, b):
    return lax.dot_general(a, b, (((1,), (1,)), ((), ())), preferred_element_type=F32)


def nn(a, b):
    return jnp.dot(a, b, preferred_element_type=F32)


def transposed(a):
    return jnp.transpose(a.astype(F32)).astype(BF)


def kernel(
    q, k, v, wo, di, pe, ct,
    dq, dk, dv, dw, dd,
    q_all, k_all, v_all, w_v, d_v, pe_v, ct_v,
    m_part, m_recv, m_own, m_all,
    vt, kt, p_t, a_loc, a_r, af, aft,
    xp, xr, gx_all, ga_f, ga_h,
    dk_acc, dv_acc, dq_b, dk_b, dv_b,
    g_send, g_own, g_r1, g2, g_r2, g3, g_r3, grow, dop, gperm, gcol, ddp, dd_r, dd_o,
    loc, qkv_s, qkv_r, mr_s, mr_r, ma_s, ma_r, my_s, my_r, mc_s, mc_r,
    a_s, a_rs, x_s, x_r, gx_s, gx_r, ga_s, ga_r, o_s, o_r,
    g1_s, g1_r, g2_s, g2_r, g3_s, g3_r, g4_s, g4_r, gc_s, gc_r, h_s, h_r,
    z_s, z_r, y_s, y_r, c_s, c_r,
):
    g, s, h = lax.axis_index("grp"), lax.axis_index("seq"), lax.axis_index("head")
    zh, y, c = g // 8, (g // 2) % 4, g % 2
    ring = (1, 2, 3)
    seq_at = lambda o: {"seq": (s + o) % 4}
    head_at = lambda o: {"head": (h + o) % 4}
    y_at = lambda o: {"grp": zh * 8 + ((y + o) % 4) * 2 + c}
    core_at = {"grp": zh * 8 + y * 2 + (1 - c)}
    zh_at = {"grp": (1 - zh) * 8 + y * 2 + c}

    def z_at(o):
        other = (zh * 4 + s + o) % 8
        return other // 4, other % 4

    sent = []

    def push(src, dst, send_sem, recv_sem, device):
        copy = pltpu.make_async_remote_copy(
            src_ref=src, dst_ref=dst, send_sem=send_sem, recv_sem=recv_sem,
            device_id=device, device_id_type=MESH,
        )
        copy.start()
        sent.append(copy)
        return copy

    def cols(index):
        return pl.ds(pl.multiple_of(index * HD, HD), HD)

    loads = [
        (wo, w_v), (di, d_v), (pe.at[0, 0], pe_v), (ct.at[0, 0], ct_v),
        (q.at[0, :, cols(s)], q_all.at[s]), (k.at[0, :, cols(s)], k_all.at[s]),
        (v.at[0, :, cols(s)], v_all.at[s]),
    ]
    loads = [pltpu.make_async_copy(src, dst, loc.at[i]) for i, (src, dst) in enumerate(loads)]
    for copy in loads:
        copy.start()

    barrier = pltpu.get_barrier_semaphore()
    greet = lambda device: pl.semaphore_signal(barrier, inc=1, device_id=device, device_id_type=MESH)
    for o in ring:
        greet(seq_at(o))
        greet(head_at(o))
        greet({"grp": (1 - zh) * 8 + y * 2 + c, "seq": (s + o) % 4})
    for o in range(1, 16):
        greet({"grp": (g + o) % 16})

    loads[0].wait()
    loads[1].wait()
    row0 = pl.multiple_of((c * 4 + y) * 64, 64)
    w_rows = w_v[pl.ds(row0, 64), :]
    for step in range(2):
        part = nn(w_rows, d_v[step])
        for half in range(2):
            m_part[2 * step + half] = part[:, half * 512 : half * 512 + 512].astype(BF)
    pl.semaphore_wait(barrier, 24)

    m_rs = [
        push(m_part.at[(s + o) % 4], m_recv.at[o - 1], mr_s.at[o - 1], mr_r.at[o - 1], seq_at(o))
        for o in ring
    ]
    qkv = []
    for n, (src, dst) in enumerate(((k, k_all), (q, q_all), (v, v_all))):
        for o in ring:
            qkv.append(
                push(
                    src.at[0, :, cols((s + o) % 4)], dst.at[s],
                    qkv_s.at[n * 3 + o - 1], qkv_r.at[n * 3 + o - 1], seq_at(o),
                )
            )

    for copy in m_rs:
        copy.wait_recv()
    total = m_part[s].astype(F32)
    for o in ring:
        total += m_recv[o - 1].astype(F32)
    m_own[...] = total.astype(BF)
    m_all[s, pl.ds(row0, 64), :] = m_own[...]
    m_ag = [
        push(m_own, m_all.at[s, pl.ds(row0, 64), :], ma_s.at[o - 1], ma_r.at[o - 1], seq_at(o))
        for o in ring
    ]
    for copy in m_ag:
        copy.wait_recv()
    rows = m_all.at[:, pl.ds(row0, 64), :]
    m_ys = [push(rows, rows, my_s.at[o - 1], my_r.at[o - 1], y_at(o)) for o in ring]

    for copy in loads[2:]:
        copy.wait()
    for copy in qkv:
        copy.wait_recv()
    for i in range(4):
        vt[:, i * 256 : i * 256 + 256] = transposed(v_all[i])
        kt[:, i * 256 : i * 256 + 256] = transposed(k_all[i])
    visible = lax.broadcasted_iota(jnp.int32, (256, 256), 0) <= lax.broadcasted_iota(
        jnp.int32, (256, 256), 1
    )
    a_cp = []
    for i in range(4):
        kk = (i + 1) * 256
        st = nt(k_all[0 : i + 1].reshape(kk, HD), q_all[i])
        diagonal = jnp.where(visible, st[i * 256 :], -1e30)
        st = diagonal if i == 0 else jnp.concatenate([st[: i * 256], diagonal], axis=0)
        top = jnp.max(st, axis=0, keepdims=True)
        e = jnp.exp2((st - top) * (SCALE * LOG2E))
        inverse = 1.0 / jnp.sum(e, axis=0, keepdims=True)
        p = (e * inverse).astype(BF)
        p_t[i, 0:kk] = p
        a_loc[i] = jnp.transpose(nn(vt[:, 0:kk], p)).astype(BF).reshape(4, 64, HD)
        a_r[i, s] = a_loc[i, s]
        for o in ring:
            at = i * 3 + o - 1
            a_cp.append(
                push(a_loc.at[i, (s + o) % 4], a_r.at[i, s], a_s.at[at], a_rs.at[at], seq_at(o))
            )

    for copy in m_ys:
        copy.wait_recv()
    half = m_all.at[:, pl.ds(pl.multiple_of(c * 256, 256), 256), :]
    m_c = push(half, half, mc_s, mc_r, core_at)

    for copy in a_cp:
        copy.wait_recv()
    for i in range(4):
        for src in range(4):
            af[i * 64 : i * 64 + 64, src * HD : src * HD + HD] = a_r[i, src]
    m_c.wait_recv()

    for t in range(4):
        xp[:, :, t * 512 : t * 512 + 512] = nn(af[...], m_all[t]).astype(BF).reshape(4, 64, 512)
    x_cp = [
        push(xp.at[(h + o) % 4], xr.at[o - 1], x_s.at[o - 1], x_r.at[o - 1], head_at(o))
        for o in ring
    ]
    for i in range(2):
        aft[i] = transposed(af[:, i * 256 : i * 256 + 256])
    for copy in x_cp:
        copy.wait_recv()
    for step in range(2):
        at = slice(step * 1024, step * 1024 + 1024)
        x = xp[h, :, at].astype(F32)
        for o in ring:
            x += xr[o - 1, :, at].astype(F32)
        x += pe_v[:, at].astype(F32)
        r = lax.rsqrt(jnp.mean(x * x, axis=-1, keepdims=True) + 1e-05)
        normed = x * r
        co = ct_v[:, at].astype(F32)
        gx = r * (co - normed * jnp.mean(co * normed, axis=-1, keepdims=True))
        gx_all[h, :, at] = gx.astype(BF)
    gx_cp = [
        push(gx_all.at[h], gx_all.at[h], gx_s.at[o - 1], gx_r.at[o - 1], head_at(o)) for o in ring
    ]
    for copy in gx_cp:
        copy.wait_recv()

    ga = jnp.zeros((256, 512), F32)
    for t in range(4):
        ga += nt(gx_all[:, :, t * 512 : t * 512 + 512].reshape(256, 512), m_all[t])
    for src in range(4):
        ga_f[src] = ga[:, src * HD : src * HD + HD].astype(BF).reshape(4, 64, HD)
    ga_h[:, s] = ga_f[s]
    ga_cp = [
        push(ga_f.at[(s + o) % 4], ga_h.at[:, s], ga_s.at[o - 1], ga_r.at[o - 1], seq_at(o))
        for o in ring
    ]
    for t in range(4):
        at = slice(t * 512, t * 512 + 512)
        g_send[:, at] = nn(aft[1 - c], gx_all[:, :, at].reshape(256, 512)).astype(BF)
    g1 = push(g_send, g_r1, g1_s, g1_r, core_at)
    for t in range(4):
        at = slice(t * 512, t * 512 + 512)
        g_own[:, at] = nn(aft[c], gx_all[:, :, at].reshape(256, 512))

    for copy in ga_cp:
        copy.wait_recv()

    out_cp = []

    def backward(i):
        kk = (i + 1) * 256
        ga_i = ga_h[i].reshape(256, HD)
        dpt = nt(v_all[0 : i + 1].reshape(kk, HD), ga_i)
        a_i = a_loc[i].reshape(256, HD)
        delta = jnp.sum(jnp.transpose(ga_i.astype(F32) * a_i.astype(F32)), axis=0, keepdims=True)
        p = p_t[i, 0:kk]
        ds = (p.astype(F32) * (dpt - delta)).astype(BF)
        dv_i, dk_i = nn(p, ga_i), nn(ds, q_all[i])
        if i == 3:
            dv_acc[...] = dv_i
            dk_acc[...] = dk_i
        else:
            dv_acc[0:kk] += dv_i
            dk_acc[0:kk] += dk_i
        dq_b[i] = (jnp.transpose(nn(kt[:, 0:kk], ds)) * SCALE).astype(BF)
        dk_b[i] = (dk_acc[i * 256 : kk] * SCALE).astype(BF)
        dv_b[i] = dv_acc[i * 256 : kk].astype(BF)

        outs = ((dq_b, dq), (dk_b, dk), (dv_b, dv))
        o = (i - s + 4) % 4
        remote, local = [], []
        for n, (src, dst) in enumerate(outs):
            remote.append(
                pltpu.make_async_remote_copy(
                    src_ref=src.at[i], dst_ref=dst.at[0, :, cols(s)],
                    send_sem=o_s.at[n * 4 + i], recv_sem=o_r.at[n * 4 + o],
                    device_id={"seq": i}, device_id_type=MESH,
                )
            )
            local.append(
                pltpu.make_async_copy(src.at[i], dst.at[0, :, cols(s)], o_s.at[n * 4 + i])
            )

        @pl.when(s != i)
        def _():
            for copy in remote:
                copy.start()

        @pl.when(s == i)
        def _():
            for copy in local:
                copy.start()

        out_cp.append((i, remote, local))

    backward(3)
    g1.wait_recv()
    g2[...] = (g_own[...] + g_r1[...].astype(F32)).astype(BF).reshape(4, 64, 2048)
    g2c = [
        push(g2.at[(y + o) % 4], g_r2.at[o - 1], g2_s.at[o - 1], g2_r.at[o - 1], y_at(o))
        for o in ring
    ]
    backward(2)
    backward(1)
    backward(0)

    for copy in g2c:
        copy.wait_recv()
    total = g2[y].astype(F32)
    for o in ring:
        total += g_r2[o - 1].astype(F32)
    for t in range(4):
        g3[:, t] = total[:, t * 512 : t * 512 + 512].astype(BF).reshape(2, 32, 512)
    g3c = []
    for o in range(1, 8):
        oz, os = z_at(o)
        g3c.append(
            push(
                g3.at[oz, os], g_r3.at[o - 1], g3_s.at[o - 1], g3_r.at[o - 1],
                {"grp": oz * 8 + y * 2 + c, "seq": os},
            )
        )
    for copy in g3c:
        copy.wait_recv()
    total = g3[zh, s].astype(F32)
    for o in range(1, 8):
        total += g_r3[o - 1].astype(F32)
    grow[s] = total.astype(BF)
    g4c = [push(grow.at[s], grow.at[s], g4_s.at[o - 1], g4_r.at[o - 1], seq_at(o)) for o in ring]
    for copy in g4c:
        copy.wait_recv()

    block = c * 8 + y * 2 + zh
    for j in range(16):
        t, at = j // 8, (j % 8) * 64
        gperm[j] = jnp.concatenate([grow[t, :, at : at + 64], grow[2 + t, :, at : at + 64]], axis=1)
    gcol[block] = gperm[g]
    gcc = [
        push(
            gperm.at[(g + o) % 16], gcol.at[block], gc_s.at[o - 1], gc_r.at[o - 1],
            {"grp": (g + o) % 16},
        )
        for o in range(1, 16)
    ]
    mine = jnp.zeros((32, 1024), F32)
    for t in range(4):
        mine += nt(grow[t], d_v[t // 2, :, (t % 2) * 512 : (t % 2) * 512 + 512])
    out_rows = dop.at[pl.ds(pl.multiple_of(block * 32, 32), 32)]
    out_rows[...] = mine.astype(BF)
    z1 = push(out_rows, out_rows, z_s, z_r, zh_at)

    for copy in gcc:
        copy.wait_recv()
    gct = transposed(gcol[...].reshape(512, HD))
    for j in range(4):
        ddp[j] = nn(gct, w_v[:, j * 256 : j * 256 + 256]).astype(BF)
    hc = [
        push(ddp.at[(h + o) % 4], dd_r.at[o - 1], h_s.at[o - 1], h_r.at[o - 1], head_at(o))
        for o in ring
    ]

    z1.wait_recv()
    rows = dop.at[pl.ds(pl.multiple_of((c * 4 + y) * 64, 64), 64)]
    y1 = [push(rows, rows, y_s.at[o - 1], y_r.at[o - 1], y_at(o)) for o in ring]
    for copy in hc:
        copy.wait_recv()
    total = ddp[h].astype(F32)
    for o in ring:
        total += dd_r[o - 1].astype(F32)
    dd_o[...] = jnp.transpose(total)
    dd_c = pltpu.make_async_copy(dd_o, dd, loc.at[7])
    dd_c.start()
    for copy in y1:
        copy.wait_recv()
    core_rows = pl.ds(pl.multiple_of(c * 256, 256), 256)
    c1 = push(dop.at[core_rows], dw.at[core_rows], c_s, c_r, core_at)
    dw_c = pltpu.make_async_copy(dop.at[core_rows], dw.at[core_rows], loc.at[8])
    dw_c.start()

    for i, remote, local in out_cp:

        @pl.when(s != i)
        def _():
            for copy in remote:
                copy.wait_send()

        @pl.when(s == i)
        def _():
            for copy in local:
                copy.wait()

    for n, (src, dst) in enumerate(((dq_b, dq), (dk_b, dk), (dv_b, dv))):
        for o in ring:
            pltpu.make_async_remote_copy(
                src_ref=src.at[0], dst_ref=dst.at[0, :, cols(s)],
                send_sem=o_s.at[n * 4], recv_sem=o_r.at[n * 4 + o],
                device_id=seq_at(o), device_id_type=MESH,
            ).wait_recv()
    c1.wait_recv()
    dw_c.wait()
    dd_c.wait()
    for copy in sent:
        copy.wait_send()


def shards(t_query, t_key, t_value, out_proj, depth_in, prev_embed, cotangent):
    prev = prev_embed.reshape(1, 1, 64, 2048)
    cot = cotangent.reshape(1, 1, 64, 2048)
    vmem = lambda shape, kind=BF: pltpu.VMEM(shape, kind)
    dma = lambda *n: pltpu.SemaphoreType.DMA(n)
    frames = jax.ShapeDtypeStruct((1, 256, 512), BF)
    dq, dk, dv, dw, dd = pl.pallas_call(
        kernel,
        out_shape=(
            frames, frames, frames,
            jax.ShapeDtypeStruct((512, 1024), BF), jax.ShapeDtypeStruct((256, 128), F32),
        ),
        in_specs=[pl.BlockSpec(memory_space=pl.ANY)] * 7,
        out_specs=[pl.BlockSpec(memory_space=pl.ANY)] * 5,
        scratch_shapes=[
            vmem((4, 256, HD)), vmem((4, 256, HD)), vmem((4, 256, HD)),
            vmem((512, 1024)), vmem((2, 1024, 1024)), vmem((64, 2048)), vmem((64, 2048)),
            vmem((4, 64, 512)), vmem((3, 64, 512)), vmem((64, 512)), vmem((4, 512, 512)),
            vmem((HD, 1024)), vmem((HD, 1024)), vmem((4, 1024, 256)),
            vmem((4, 4, 64, HD)), vmem((4, 4, 64, HD)), vmem((256, 512)), vmem((2, 256, 256)),
            vmem((4, 64, 2048)), vmem((3, 64, 2048)), vmem((4, 64, 2048)),
            vmem((4, 4, 64, HD)), vmem((4, 4, 64, HD)),
            vmem((1024, HD), F32), vmem((1024, HD), F32),
            vmem((4, 256, HD)), vmem((4, 256, HD)), vmem((4, 256, HD)),
            vmem((256, 2048)), vmem((256, 2048), F32), vmem((256, 2048)),
            vmem((4, 64, 2048)), vmem((3, 64, 2048)), vmem((2, 4, 32, 512)), vmem((7, 32, 512)),
            vmem((4, 32, 512)), vmem((512, 1024)), vmem((16, 32, HD)), vmem((16, 32, HD)),
            vmem((4, HD, 256)), vmem((3, HD, 256)), vmem((256, HD), F32),
            dma(9), dma(9), dma(9), dma(3), dma(3), dma(3), dma(3), dma(3), dma(3), dma(), dma(),
            dma(12), dma(12), dma(3), dma(3), dma(3), dma(3), dma(3), dma(3), dma(12), dma(12),
            dma(), dma(), dma(3), dma(3), dma(7), dma(7), dma(3), dma(3), dma(15), dma(15),
            dma(3), dma(3), dma(), dma(), dma(3), dma(3), dma(), dma(),
        ],
        compiler_params=pltpu.CompilerParams(
            collective_id=0, has_side_effects=True, vmem_limit_bytes=48 * 1024 * 1024
        ),
    )(t_query, t_key, t_value, out_proj, depth_in, prev, cot)
    grad_depth = jnp.transpose(dd.reshape(256, 2, 64), (1, 0, 2))
    return dq.astype(F32), dk.astype(F32), dv.astype(F32), dw.astype(F32), grad_depth


def solution(mesh):
    placed = (
        P("grp", "seq", "head"),
        P("grp", "seq", "head"),
        P("grp", "seq", "head"),
        P("head", "seq"),
        P(None, "seq", None),
        P("grp", "head", "seq", None, None),
        P("grp", "head", "seq", None, None),
    )
    return jax.shard_map(
        shards,
        mesh=mesh,
        in_specs=placed,
        out_specs=(
            P("grp", "seq", "head"),
            P("grp", "seq", "head"),
            P("grp", "seq", "head"),
            P("head", "seq"),
            P(None, ("seq", "head"), "grp"),
        ),
        check_vma=False,
    )
```

time: 749 us -> 158 us (0.21)
  waiting for transfers between devices: 662 us -> 0 us
  Pallas kernels: 0 us -> 146 us
  matrix products: 46.3 us -> 0 us
  between operations: 14.1 us -> 0.66 us
  other arithmetic: 13.8 us -> 4.13 us
    reduce_scatter x7 -> x0, waiting for transfers between devices: 328 us -> none  [the longest x1 99 us: shards(): lax.psum_scatter(win_terms.astype(jnp.bfloat16), 'grp', scatter_dimension...]
    psum x1 -> x0, waiting for transfers between devices: 167 us -> none  [shards(): lax.psum(wo_terms.astype(jnp.bfloat16), 'grp').astype(jnp.float32)]
    all_gather x5 -> x0, waiting for transfers between devices: 165 us -> none  [the longest x1 39.4 us: shards(): lax.all_gather(t_key[0], 'seq', axis=0, tiled=True)]
    pallas_call x0 -> x1, Pallas kernels: none -> 146 us  [shards(): pl.pallas_call(kernel, out_shape=(frames, frames, frames, jax.ShapeDtypeS...]
    dot_general x11 -> x0, matrix products: 41.2 us -> none  [the longest x1 5.08 us: shards(): jnp.einsum('fd,kdc->fkc', context, depth_in, preferred_element_type=jnp.f...]
  transfers between devices with their start and end apart: 13 -> 0, of which waited for: 13 -> 0; matrix products, arithmetic and copies ran while one was open for 6% -> 0% of each run, Pallas kernels for 0% -> 0%
where the time goes in v1:
time: 158 us
  Pallas kernels  146 us (92%)
  local copies, waits for them, and re-layouts  7.09 us (4%)
  other arithmetic  4.13 us (3%)
    pallas_call x1, Pallas kernels, shards(): pl.pallas_call(kernel, out_shape=(frames, frames, frames, jax.ShapeDtypeS...  146 us
    unnamed x8, local copies, waits for them, and re-layouts  4.07 us

profile of v1, /device:TPU:1, one launch (start us, length us, event | category | flops | bytes accessed | tf_op | source)
XLA Modules:
  0.0 158.0 jit_solution(1624124256677261713)
XLA Ops:
  0.6 1.1 reshape.19.pe
  1.8 1.1 reshape.20.ct
  2.9 0.0 copy-start
  2.9 1.2 copy-done
  4.1 0.0 copy-start.1
  4.1 0.9 copy-done.1
  5.1 0.0 copy-start.2
  5.1 0.9 copy-done.2
  6.0 0.0 copy-start.3
  6.0 0.9 copy-done.3
  7.0 146.1 %shard_map.110 = (bf16[1,256,512]{2,1,0:T(8,128)(2,1)S(1)}, bf16[1,256,512]{2,1,0:T(8,128)(2,1)S(1)}, bf16[1,256,512]{2,1,0:T(8,128)(2,1)S(1)}, bf16[512,1024]{1,0:T(8,128)(2,1)S(1)}, f32[256,128]{1,0:T(8,128)S(1)}) custom-call(bf16[1,256,512]{2,1,0:T(8,128)(2,1)S(1)} %copy-done.1, bf16[1,256,512]{2,1,0:T(8,128)(2,1)S(1)} %copy-done.2, ...), custom_call_target="tpu_custom_call" | custom-call | tf_op jit(solution)/shard_map/pallas_call | solution.py:380
  153.1 1.6 convert_element_type.15
  154.7 0.9 convert_element_type.12
  155.5 0.9 convert_element_type.13
  156.4 0.9 convert_element_type.14
  157.3 0.8 copy.13
Async XLA Ops:
  2.9 1.2 copy-start
  4.1 0.9 copy-start.1
  5.1 0.9 copy-start.2
  6.0 0.9 copy-start.3

commit v2 on v1

v2 whole, which is shorter than its diff:
```python
import jax
import jax.numpy as jnp
from jax import lax
from jax.experimental import pallas as pl
from jax.experimental.pallas import tpu as pltpu
from jax.sharding import PartitionSpec as P

MESH = pl.DeviceIdType.MESH
HD = 128
BF = jnp.bfloat16
F32 = jnp.float32
SCALE = HD ** (-0.5)
LOG2E = 1.4426950408889634


def nt(a, b):
    return lax.dot_general(a, b, (((1,), (1,)), ((), ())), preferred_element_type=F32)


def nn(a, b):
    return jnp.dot(a, b, preferred_element_type=F32)


def transposed(a):
    return jnp.transpose(a.astype(F32)).astype(BF)


def kernel(
    q, k, v, wo, di, pe, ct,
    dq, dk, dv, dw, dd,
    q_all, k_all, v_all, w_v, d_v, pe_v, ct_v, pe_w, ct_w,
    m_part, m_recv, m_own, m_all,
    vt, kt, p_t, a_loc, a_r, af, aft,
    xp, x_land, gx_all, ga_f, ga_h,
    dk_acc, dv_acc, dq_b, dk_b, dv_b,
    g_send, g_r1, g2, g_land, g3, g_r3, grow, dop, gperm, gcol, ddp, dd_r, dd_o,
    loc, qkv_s, qkv_r, mr_s, mr_r, ma_s, ma_r, my_s, my_r, mc_s, mc_r,
    a_s, a_rs, x_s, x_r, gx_s, gx_r, ga_s, ga_r, o_s, o_r,
    g1_s, g1_r, g2_s, g2_r, g3_s, g3_r, g4_s, g4_r, gc_s, gc_r, h_s, h_r,
    y_s, y_r, c_s, c_r,
):
    g, s, h = lax.axis_index("grp"), lax.axis_index("seq"), lax.axis_index("head")
    zh, y, c = g // 8, (g // 2) % 4, g % 2
    ring = (1, 2, 3)
    seq_at = lambda o: {"seq": (s + o) % 4}
    head_at = lambda o: {"head": (h + o) % 4}
    y_at = lambda o: {"grp": zh * 8 + ((y + o) % 4) * 2 + c}
    core_at = {"grp": zh * 8 + y * 2 + (1 - c)}

    half_at = lambda o: {"grp": zh * 8 + (g + o) % 8}

    def z_at(o):
        other = (zh * 4 + s + o) % 8
        return other // 4, other % 4

    def z_device(o):
        oz, os = z_at(o)
        return {"grp": oz * 8 + y * 2 + c, "seq": os}

    sent = []

    def push(src, dst, send_sem, recv_sem, device):
        copy = pltpu.make_async_remote_copy(
            src_ref=src, dst_ref=dst, send_sem=send_sem, recv_sem=recv_sem,
            device_id=device, device_id_type=MESH,
        )
        copy.start()
        sent.append(copy)
        return copy

    def ring_sum(part, land, at, i, send, recv):
        right, left = (i + 1) % 4, (i + 3) % 4
        copies = {}

        def go(n, j, half, device):
            copies[n] = push(part.at[j, half], land.at[n], send.at[n], recv.at[n], device)

        def opposite():
            go(0, (i + 2) % 4, 0, at(1))
            go(1, (i + 2) % 4, 1, at(3))

        def to_left():
            go(2, left, 0, at(3))

        def to_right():
            go(3, right, 1, at(1))

        def relay():
            copies[0].wait_recv()
            part[right, 0] = (part[right, 0].astype(F32) + land[0].astype(F32)).astype(BF)
            go(4, right, 0, at(1))
            copies[1].wait_recv()
            part[left, 1] = (part[left, 1].astype(F32) + land[1].astype(F32)).astype(BF)
            go(5, left, 1, at(3))

        def result(half):
            copies[2 + half].wait_recv()
            copies[4 + half].wait_recv()
            total = part[i, half].astype(F32) + land[2 + half].astype(F32)
            return total + land[4 + half].astype(F32)

        return opposite, to_left, to_right, relay, result

    def ring_gather(view, at, i, send, recv):
        copies = {}

        def go(n, j, half, device):
            copies[n] = push(view(j, half), view(j, half), send.at[n], recv.at[n], device)

        def start(half):
            go(2 * half, i, half, at(1))
            go(2 * half + 1, i, half, at(3))

        def relay():
            copies[0].wait_recv()
            go(4, (i + 3) % 4, 0, at(1))
            copies[3].wait_recv()
            go(5, (i + 1) % 4, 1, at(3))

        return start, relay, copies

    def cols(index):
        return pl.ds(pl.multiple_of(index * HD, HD), HD)

    loads = [
        (wo, w_v), (di, d_v), (pe.at[0, 0], pe_v), (ct.at[0, 0], ct_v),
        (q.at[0, :, cols(s)], q_all.at[s]), (k.at[0, :, cols(s)], k_all.at[s]),
        (v.at[0, :, cols(s)], v_all.at[s]),
    ]
    loads = [pltpu.make_async_copy(src, dst, loc.at[i]) for i, (src, dst) in enumerate(loads)]
    for copy in loads:
        copy.start()

    barrier = pltpu.get_barrier_semaphore()
    greet = lambda device: pl.semaphore_signal(barrier, inc=1, device_id=device, device_id_type=MESH)
    for o in ring:
        greet(seq_at(o))
        greet(head_at(o))
    for o in range(1, 8):
        greet(half_at(o))
    for o in range(4):
        greet({"grp": (g + 8) % 16, "seq": (s + o) % 4})

    loads[0].wait()
    loads[1].wait()
    row0 = pl.multiple_of((c * 4 + y) * 64, 64)
    w_rows = w_v[pl.ds(row0, 64), :]
    for step in range(2):
        part = nn(w_rows, d_v[step])
        for half in range(2):
            m_part[2 * step + half] = part[:, half * 512 : half * 512 + 512].astype(BF)
    pl.semaphore_wait(barrier, 17)

    def m_spread(view, land, send, recv):
        copies = []
        for n, (o, at, rows) in enumerate(
            ((1, 1, (0, 64)), (7, 3, (0, 64)), (2, 2, (0, 32)), (6, 2, (32, 32)))
        ):
            there = land(o, rows)
            copies.append(push(view(at, rows), there, send.at[n], recv.at[n], z_device(o)))
        return copies

    m_rs = m_spread(
        lambda at, rows: m_part.at[(s + at) % 4, pl.ds(*rows)],
        lambda o, rows: m_recv.at[{1: 0, 7: 1, 2: 2, 6: 2}[o], pl.ds(*rows)],
        mr_s, mr_r,
    )
    qkv = []

    def spread(n, src, dst):
        for o in ring:
            at = n * 3 + o - 1
            there = src.at[0, :, cols((s + o) % 4)]
            qkv.append(push(there, dst.at[s], qkv_s.at[at], qkv_r.at[at], seq_at(o)))

    spread(0, k, k_all)
    for copy in m_rs:
        copy.wait_recv()
    total = m_part[s].astype(F32)
    for o in ring:
        total += m_recv[o - 1].astype(F32)
    m_own[...] = total.astype(BF)
    m_all[s, pl.ds(row0, 64), :] = m_own[...]
    m_ag = m_spread(
        lambda at, rows: m_own.at[pl.ds(*rows)],
        lambda o, rows: m_all.at[s, pl.ds(pl.multiple_of(row0 + rows[0], 32), rows[1])],
        ma_s, ma_r,
    )
    spread(1, q, q_all)
    spread(2, v, v_all)
    for copy in m_ag:
        copy.wait_recv()
    def m_rows(index):
        return pl.ds(pl.multiple_of((c * 4 + index) * 64, 64), 64)

    m_start, m_relay, m_y = ring_gather(
        lambda j, half: m_all.at[2 * half : 2 * half + 2, m_rows(j)], y_at, y, my_s, my_r
    )
    m_start(0)
    m_start(1)
    m_c = []

    def m_across(n, index):
        there = m_all.at[:, m_rows(index)]
        m_c.append(push(there, there, mc_s.at[n], mc_r.at[n], core_at))

    m_across(0, y)
    m_relay()

    for copy in loads[2:]:
        copy.wait()
    for copy in qkv[:6]:
        copy.wait_recv()
    for i in range(4):
        kt[:, i * 256 : i * 256 + 256] = transposed(k_all[i])
    visible = lax.broadcasted_iota(jnp.int32, (256, 256), 0) <= lax.broadcasted_iota(
        jnp.int32, (256, 256), 1
    )
    for i in range(4):
        kk = (i + 1) * 256
        st = nt(k_all[0 : i + 1].reshape(kk, HD), q_all[i])
        diagonal = jnp.where(visible, st[i * 256 :], -1e30)
        st = diagonal if i == 0 else jnp.concatenate([st[: i * 256], diagonal], axis=0)
        top = jnp.max(st, axis=0, keepdims=True)
        e = jnp.exp2((st - top) * (SCALE * LOG2E))
        inverse = 1.0 / jnp.sum(e, axis=0, keepdims=True)
        p_t[i, 0:kk] = (e * inverse).astype(BF)
    for copy in qkv[6:]:
        copy.wait_recv()
    for i in range(4):
        vt[:, i * 256 : i * 256 + 256] = transposed(v_all[i])
    for i in range(4):
        kk = (i + 1) * 256
        a_loc[i] = jnp.transpose(nn(vt[:, 0:kk], p_t[i, 0:kk])).astype(BF).reshape(4, 64, HD)
    h_order = [(h + o) % 4 for o in (2, 3, 1, 0)]
    a_cp = []
    for n, a in enumerate(h_order):
        a_r[a, s] = a_loc[a, s]
        for o in ring:
            at = n * 3 + o - 1
            a_cp.append(
                push(a_loc.at[a, (s + o) % 4], a_r.at[a, s], a_s.at[at], a_rs.at[at], seq_at(o))
            )

    m_y[2].wait_recv()
    m_across(1, (y + 3) % 4)
    m_y[1].wait_recv()
    m_across(2, (y + 1) % 4)
    m_y[4].wait_recv()
    m_y[5].wait_recv()
    m_across(3, (y + 2) % 4)
    for copy in m_c:
        copy.wait_recv()

    x_opposite, x_left, x_right, x_relay, x_result = ring_sum(xp, x_land, head_at, h, x_s, x_r)
    for n, send in enumerate((x_opposite, x_left, x_right, None)):
        a = h_order[n]
        for copy in a_cp[3 * n : 3 * n + 3]:
            copy.wait_recv()
        for src in range(4):
            af[a, :, src * HD : src * HD + HD] = a_r[a, src]
        for t in range(4):
            there = slice((t % 2) * 512, (t % 2) * 512 + 512)
            xp[a, t // 2, :, there] = nn(af[a], m_all[t]).astype(BF)
        if send is not None:
            send()
    x_relay()
    for step in range(2):
        pe_w[step] = pe_v[:, step, :].astype(F32)
        ct_w[step] = ct_v[:, step, :].astype(F32)
    for i in range(2):
        at = transposed(af[:, :, i * 256 : i * 256 + 256].reshape(256, 256))
        aft[i] = at.reshape(4, 64, 256)
    gx_start, gx_relay, gx_cp = ring_gather(
        lambda j, half: gx_all.at[j, half], head_at, h, gx_s, gx_r
    )
    for step in range(2):
        x = x_result(step) + pe_w[step]
        r = lax.rsqrt(jnp.mean(x * x, axis=-1, keepdims=True) + 1e-05)
        normed = x * r
        co = ct_w[step]
        gx = r * (co - normed * jnp.mean(co * normed, axis=-1, keepdims=True))
        gx_all[h, step] = gx.astype(BF)
        gx_start(step)

    ga_cp = []

    def grad_rows(n, a):
        ga = jnp.zeros((64, 512), F32)
        for t in range(4):
            there = slice((t % 2) * 512, (t % 2) * 512 + 512)
            ga += nt(gx_all[a, t // 2, :, there], m_all[t])
        for src in range(4):
            ga_f[a, src] = ga[:, src * HD : src * HD + HD].astype(BF)
        ga_h[a, s] = ga_f[a, s]
        for o in ring:
            at = n * 3 + o - 1
            ga_cp.append(
                push(ga_f.at[a, (s + o) % 4], ga_h.at[a, s], ga_s.at[at], ga_r.at[at], seq_at(o))
            )

    grad_rows(0, h)
    gx_relay()
    gx_cp[2].wait_recv()
    grad_rows(1, (h + 3) % 4)
    gx_cp[1].wait_recv()
    grad_rows(2, (h + 1) % 4)
    gx_cp[4].wait_recv()
    gx_cp[5].wait_recv()
    grad_rows(3, (h + 2) % 4)

    y_order = [(y + o) % 4 for o in (2, 3, 1, 0)]

    def g_rows(core, index, step):
        return nn(aft[core, index], gx_all[:, step].reshape(256, 1024))

    g1 = []
    for n, index in enumerate(y_order):
        for step in range(2):
            g_send[index, step] = g_rows(1 - c, index, step).astype(BF)
        g1.append(push(g_send.at[index], g_r1.at[index], g1_s.at[n], g1_r.at[n], core_at))

    g_opposite, g_left, g_right, g_relay, g_result = ring_sum(g2, g_land, y_at, y, g2_s, g2_r)
    for n, send in enumerate((g_opposite, g_left, g_right, None)):
        index = y_order[n]
        own = [g_rows(c, index, step) for step in range(2)]
        g1[n].wait_recv()
        for step in range(2):
            g2[index, step] = (own[step] + g_r1[index, step].astype(F32)).astype(BF)
        if send is not None:
            send()

    for copy in ga_cp:
        copy.wait_recv()

    def backward(i):
        kk = (i + 1) * 256
        ga_i = ga_h[i].reshape(256, HD)
        dpt = nt(v_all[0 : i + 1].reshape(kk, HD), ga_i)
        a_i = a_loc[i].reshape(256, HD)
        delta = jnp.sum(jnp.transpose(ga_i.astype(F32) * a_i.astype(F32)), axis=0, keepdims=True)
        p = p_t[i, 0:kk]
        ds = (p.astype(F32) * (dpt - delta)).astype(BF)
        dv_i, dk_i = nn(p, ga_i), nn(ds, q_all[i])
        if i == 3:
            dv_acc[...] = dv_i
            dk_acc[...] = dk_i
        else:
            dv_acc[0:kk] += dv_i
            dk_acc[0:kk] += dk_i
        dq_b[i] = (jnp.transpose(nn(kt[:, 0:kk], ds)) * SCALE).astype(BF)
        dk_b[i] = (dk_acc[i * 256 : kk] * SCALE).astype(BF)
        dv_b[i] = dv_acc[i * 256 : kk].astype(BF)


    for i in (3, 2, 1, 0):
        backward(i)
    outs = ((dq_b, dq), (dk_b, dk), (dv_b, dv))
    out_cp, out_own = [], []

    def give(n):
        src, dst = outs[n]
        there = dst.at[0, :, cols(s)]
        for o in ring:
            at = n * 3 + o - 1
            out_cp.append(push(src.at[(s + o) % 4], there, o_s.at[at], o_r.at[at], seq_at(o)))
        out_own.append(pltpu.make_async_copy(src.at[s], there, loc.at[16 + n]))
        out_own[-1].start()

    give(0)
    g_relay()
    give(1)
    for step in range(2):
        total = g_result(step)
        for t in range(2):
            there = total[:, t * 512 : t * 512 + 512].astype(BF)
            g3[:, 2 * step + t] = there.reshape(2, 32, 512)
    g3c = []
    for o in range(1, 8):
        oz, os = z_at(o)
        g3c.append(
            push(g3.at[oz, os], g_r3.at[o - 1], g3_s.at[o - 1], g3_r.at[o - 1], z_device(o))
        )
    for copy in g3c:
        copy.wait_recv()
    total = g3[zh, s].astype(F32)
    for o in range(1, 8):
        total += g_r3[o - 1].astype(F32)
    grow[s, zh] = total.astype(BF)
    g4c = [
        push(grow.at[s, zh], grow.at[s, zh], g4_s.at[o - 1], g4_r.at[o - 1], z_device(o))
        for o in range(1, 8)
    ]
    give(2)
    for copy in g4c:
        copy.wait_recv()

    for j in range(8):
        there = slice(j * 64, j * 64 + 64)
        pair = [grow[2 * step + zh, :, :, there].reshape(64, 64) for step in range(2)]
        gperm[j] = jnp.concatenate(pair, axis=1)
    block = c * 4 + y
    gcol[block] = gperm[g % 8]
    gcc = [
        push(
            gperm.at[(g + o) % 8], gcol.at[block], gc_s.at[o - 1], gc_r.at[o - 1], half_at(o)
        )
        for o in range(1, 8)
    ]
    y_cp = []
    for half in range(2):
        mine = jnp.zeros((64, 512), F32)
        for t in range(4):
            depth = d_v[t // 2, half * 512 : half * 512 + 512, (t % 2) * 512 : (t % 2) * 512 + 512]
            mine += nt(grow[t].reshape(64, 512), depth)
        dop[half, m_rows(y)] = mine.astype(BF)
        here = dop.at[half, m_rows(y)]
        for o in ring:
            at = half * 3 + o - 1
            y_cp.append(push(here, here, y_s.at[at], y_r.at[at], y_at(o)))

    c1, dw_c = [], []

    def out_across(n, index):
        for half in range(2):
            at = 2 * n + half
            if n:
                y_cp[half * 3 + n - 1].wait_recv()
            here = dop.at[half, m_rows(index)]
            there = dw.at[m_rows(index), half * 512 : half * 512 + 512]
            dw_c.append(pltpu.make_async_copy(here, there, loc.at[8 + at]))
            dw_c[at].start()
            c1.append(push(here, there, c_s.at[at], c_r.at[at], core_at))

    out_across(0, y)
    for copy in gcc:
        copy.wait_recv()
    gct = transposed(gcol[...].reshape(512, HD))
    for j in range(4):
        ddp[j] = nn(gct, w_v[:, j * 256 : j * 256 + 256]).astype(BF)
    hc = [
        push(ddp.at[(h + o) % 4], dd_r.at[o - 1], h_s.at[o - 1], h_r.at[o - 1], head_at(o))
        for o in ring
    ]
    for o in ring:
        out_across(o, (y + 4 - o) % 4)
    for copy in hc:
        copy.wait_recv()
    total = ddp[h].astype(F32)
    for o in ring:
        total += dd_r[o - 1].astype(F32)
    dd_o[...] = total
    dd_c = pltpu.make_async_copy(dd_o, dd, loc.at[7])
    dd_c.start()
    for copy in out_cp:
        copy.wait_recv()
    for copy in out_own:
        copy.wait()
    for copy in c1:
        copy.wait_recv()
    for copy in dw_c:
        copy.wait()
    dd_c.wait()
    for copy in sent:
        copy.wait_send()


def widen(dq, dk, dv, dw, dd, *refs):
    outs, (narrow, tokens, weight, load, store) = refs[:5], refs[5:]
    parts = [(src.at[0], dst.at[0], tokens.at[n]) for n, (src, dst) in enumerate(zip((dq, dk, dv), outs))]
    for n in range(4):
        rows = slice(n * 128, n * 128 + 128)
        for half in range(2):
            at = (rows, slice(half * 512, half * 512 + 512))
            parts.append((dw.at[at], outs[3].at[at], weight.at[n, half]))
    held = [narrow.at[n] if n < 3 else narrow.at[n, 0:128] for n in range(11)]
    loads = [pltpu.make_async_copy(p[0], held[n], load.at[n]) for n, p in enumerate(parts)]
    stores = [pltpu.make_async_copy(p[2], p[1], store.at[n]) for n, p in enumerate(parts)]
    stores.append(pltpu.make_async_copy(dd, outs[4], store.at[11]))
    stores[11].start()
    for copy in loads:
        copy.start()
    for n, part in enumerate(parts):
        loads[n].wait()
        part[2][...] = held[n][...].astype(F32)
        stores[n].start()
    for copy in stores:
        copy.wait()


def shards(t_query, t_key, t_value, out_proj, depth_in, prev_embed, cotangent):
    vmem = lambda shape, kind=BF: pltpu.VMEM(shape, kind)
    dma = lambda *n: pltpu.SemaphoreType.DMA(n)
    frames = jax.ShapeDtypeStruct((1, 256, 512), BF)
    dq, dk, dv, dw, dd = pl.pallas_call(
        kernel,
        out_shape=(
            frames, frames, frames,
            jax.ShapeDtypeStruct((512, 1024), BF), jax.ShapeDtypeStruct((HD, 256), F32),
        ),
        in_specs=[pl.BlockSpec(memory_space=pl.ANY)] * 7,
        out_specs=[pl.BlockSpec(memory_space=pl.ANY)] * 5,
        scratch_shapes=[
            vmem((4, 256, HD)), vmem((4, 256, HD)), vmem((4, 256, HD)),
            vmem((512, 1024)), vmem((2, 1024, 1024)), vmem((64, 2, 1024)), vmem((64, 2, 1024)),
            vmem((2, 64, 1024), F32), vmem((2, 64, 1024), F32),
            vmem((4, 64, 512)), vmem((3, 64, 512)), vmem((64, 512)), vmem((4, 512, 512)),
            vmem((HD, 1024)), vmem((HD, 1024)), vmem((4, 1024, 256)),
            vmem((4, 4, 64, HD)), vmem((4, 4, 64, HD)), vmem((4, 64, 512)), vmem((2, 4, 64, 256)),
            vmem((4, 2, 64, 1024)), vmem((6, 64, 1024)), vmem((4, 2, 64, 1024)),
            vmem((4, 4, 64, HD)), vmem((4, 4, 64, HD)),
            vmem((1024, HD), F32), vmem((1024, HD), F32),
            vmem((4, 256, HD)), vmem((4, 256, HD)), vmem((4, 256, HD)),
            vmem((4, 2, 64, 1024)), vmem((4, 2, 64, 1024)), vmem((4, 2, 64, 1024)),
            vmem((6, 64, 1024)), vmem((2, 4, 32, 512)), vmem((7, 32, 512)),
            vmem((4, 2, 32, 512)), vmem((2, 512, 512)), vmem((8, 64, HD)), vmem((8, 64, HD)),
            vmem((4, HD, 256)), vmem((3, HD, 256)), vmem((HD, 256), F32),
            dma(19), dma(9), dma(9), dma(4), dma(4), dma(4), dma(4), dma(6), dma(6), dma(4), dma(4),
            dma(12), dma(12), dma(6), dma(6), dma(6), dma(6), dma(12), dma(12), dma(9), dma(9),
            dma(4), dma(4), dma(6), dma(6), dma(7), dma(7), dma(7), dma(7), dma(7), dma(7),
            dma(3), dma(3), dma(6), dma(6), dma(8), dma(8),
        ],
        compiler_params=pltpu.CompilerParams(
            collective_id=0, has_side_effects=True, vmem_limit_bytes=60 * 1024 * 1024
        ),
    )(t_query, t_key, t_value, out_proj, depth_in, prev_embed, cotangent)
    wide = lambda *shape: jax.ShapeDtypeStruct(shape, F32)
    dq, dk, dv, dw, dd = pl.pallas_call(
        widen,
        out_shape=(wide(1, 256, 512), wide(1, 256, 512), wide(1, 256, 512), wide(512, 1024), wide(HD, 256)),
        in_specs=[pl.BlockSpec(memory_space=pl.ANY)] * 5,
        out_specs=[pl.BlockSpec(memory_space=pl.ANY)] * 5,
        scratch_shapes=[
            vmem((11, 256, 512)), vmem((3, 256, 512), F32), vmem((4, 2, 128, 512), F32), dma(11), dma(12),
        ],
        compiler_params=pltpu.CompilerParams(vmem_limit_bytes=60 * 1024 * 1024),
    )(dq, dk, dv, dw, dd)
    return dq, dk, dv, dw, jnp.transpose(dd.reshape(2, 64, 256), (0, 2, 1))


def solution(mesh):
    placed = (
        P("grp", "seq", "head"),
        P("grp", "seq", "head"),
        P("grp", "seq", "head"),
        P("head", "seq"),
        P(None, "seq", None),
        P("grp", "head", "seq", None, None),
        P("grp", "head", "seq", None, None),
    )
    return jax.shard_map(
        shards,
        mesh=mesh,
        in_specs=placed,
        out_specs=(
            P("grp", "seq", "head"),
            P("grp", "seq", "head"),
            P("grp", "seq", "head"),
            P("head", "seq"),
            P(None, ("seq", "head"), "grp"),
        ),
        check_vma=False,
    )
```

time: 158 us -> 118 us (0.75)
  Pallas kernels: 146 us -> 117 us
  local copies, waits for them, and re-layouts: 7.09 us -> 0 us
  other arithmetic: 4.13 us -> 0 us
    pallas_call x1, Pallas kernels: 146 us -> 112 us  [shards(): pl.pallas_call(kernel, out_shape=(frames, frames, frames, jax.ShapeDtypeS...]
    pallas_call x0 -> x1, Pallas kernels: none -> 5.28 us  [shards(): pl.pallas_call(widen, out_shape=(wide(1, 256, 512), wide(1, 256, 512), wi...]
    convert_element_type x4 -> x0, other arithmetic: 4.13 us -> none  [the longest x1 1.57 us: shards(): dw.astype(F32)]
    unnamed x8 -> x0, local copies, waits for them, and re-layouts: 4.07 us -> none
    reshape x2 -> x0, local copies, waits for them, and re-layouts: 2.27 us -> none  [the longest x1 1.13 us: shards(): cot = cotangent.reshape(1, 1, 64, 2048)]
where the time goes in v2:
time: 118 us
  Pallas kernels  117 us (99%)
    pallas_call x1, Pallas kernels, shards(): pl.pallas_call(kernel, out_shape=(frames, frames, frames, jax.ShapeDtypeS...  112 us
    pallas_call x1, Pallas kernels, shards(): pl.pallas_call(widen, out_shape=(wide(1, 256, 512), wide(1, 256, 512), wi...  5.28 us

profile of v2, /device:TPU:1, one launch (start us, length us, event | category | flops | bytes accessed | tf_op | source)
XLA Modules:
  0.0 117.6 jit_solution(14535454228414939084)
XLA Ops:
  0.6 111.7 %shard_map.110 = (bf16[1,256,512]{2,1,0:T(8,128)(2,1)}, bf16[1,256,512]{2,1,0:T(8,128)(2,1)}, bf16[1,256,512]{2,1,0:T(8,128)(2,1)}, bf16[512,1024]{1,0:T(8,128)(2,1)}, f32[128,256]{1,0:T(8,128)}) custom-call(bf16[1,256,512]{2,1,0:T(8,128)(2,1)} %q.1, bf16[1,256,512]{2,1,0:T(8,128)(2,1)} %k.1, bf16[1,256,512]{2,1,0:T(8,128)(2,1)} %v.1, bf16[512,1024]{1,0:T(8,128)(2,1)} %wo.1, ...), custom_call_target="tpu_custom_call" | custom-call | tf_op jit(solution)/shard_map/pallas_call | solution.py:495
  112.4 5.3 %shard_map.111 = (f32[1,256,512]{2,1,0:T(8,128)}, f32[1,256,512]{2,1,0:T(8,128)}, f32[1,256,512]{2,1,0:T(8,128)}, f32[512,1024]{1,0:T(8,128)}, f32[128,256]{1,0:T(8,128)}) custom-call(bf16[1,256,512]{2,1,0:T(8,128)(2,1)} %get-tuple-element.15.dq, bf16[1,256,512]{2,1,0:T(8,128)(2,1)} %get-tuple-element.16.dk, bf16[1,256,512]{2,1,0:T(8,128)(2,1)} %get-tuple-element.17.dv, ...), custom_call_target="tpu_custom_call" | custom-call | tf_op jit(solution)/shard_map/pallas_call | solution.py:528

commit v3 on v2

--- a/solution.py
+++ b/solution.py
@@ -68,12 +68,17 @@
         sent.append(copy)
         return copy
 
-    def ring_sum(part, land, at, i, send, recv):
+    def ring_sum(view, land, at, i, send, recv):
         right, left = (i + 1) % 4, (i + 3) % 4
         copies = {}
 
         def go(n, j, half, device):
-            copies[n] = push(part.at[j, half], land.at[n], send.at[n], recv.at[n], device)
+            copies[n] = push(view(j, half), land.at[n], send.at[n], recv.at[n], device)
+
+        def add(n, j, half):
+            copies[n].wait_recv()
+            here = view(j, half)
+            here[...] = (here[...].astype(F32) + land[n].astype(F32)).astype(BF)
 
         def opposite():
             go(0, (i + 2) % 4, 0, at(1))
@@ -86,17 +91,15 @@
             go(3, right, 1, at(1))
 
         def relay():
-            copies[0].wait_recv()
-            part[right, 0] = (part[right, 0].astype(F32) + land[0].astype(F32)).astype(BF)
+            add(0, right, 0)
             go(4, right, 0, at(1))
-            copies[1].wait_recv()
-            part[left, 1] = (part[left, 1].astype(F32) + land[1].astype(F32)).astype(BF)
+            add(1, left, 1)
             go(5, left, 1, at(3))
 
         def result(half):
             copies[2 + half].wait_recv()
             copies[4 + half].wait_recv()
-            total = part[i, half].astype(F32) + land[2 + half].astype(F32)
+            total = view(i, half)[...].astype(F32) + land[2 + half].astype(F32)
             return total + land[4 + half].astype(F32)
 
         return opposite, to_left, to_right, relay, result
@@ -187,25 +190,41 @@
         ma_s, ma_r,
     )
     spread(1, q, q_all)
+    for copy in m_ag:
+        copy.wait_recv()
     spread(2, v, v_all)
-    for copy in m_ag:
-        copy.wait_recv()
     def m_rows(index):
         return pl.ds(pl.multiple_of((c * 4 + index) * 64, 64), 64)
 
-    m_start, m_relay, m_y = ring_gather(
-        lambda j, half: m_all.at[2 * half : 2 * half + 2, m_rows(j)], y_at, y, my_s, my_r
-    )
-    m_start(0)
-    m_start(1)
-    m_c = []
-
-    def m_across(n, index):
-        there = m_all.at[:, m_rows(index)]
-        m_c.append(push(there, there, mc_s.at[n], mc_r.at[n], core_at))
-
-    m_across(0, y)
-    m_relay()
+    m_rings = [
+        ring_gather(
+            lambda j, half, k=k: m_all.at[2 * k + half, m_rows(j)], y_at, y, my_s.at[k], my_r.at[k]
+        )
+        for k in range(2)
+    ]
+    for start, _, _ in m_rings:
+        start(0)
+        start(1)
+    m_c = [[], []]
+
+    def m_across(k, n, index):
+        there = m_all.at[2 * k : 2 * k + 2, m_rows(index)]
+        m_c[k].append(push(there, there, mc_s.at[4 * k + n], mc_r.at[4 * k + n], core_at))
+
+    def m_near(k):
+        m_rings[k][2][2].wait_recv()
+        m_across(k, 1, (y + 3) % 4)
+        m_rings[k][2][1].wait_recv()
+        m_across(k, 2, (y + 1) % 4)
+
+    def m_far(k):
+        m_rings[k][2][4].wait_recv()
+        m_rings[k][2][5].wait_recv()
+        m_across(k, 3, (y + 2) % 4)
+
+    for k in range(2):
+        m_across(k, 0, y)
+    m_rings[0][1]()
 
     for copy in loads[2:]:
         copy.wait()
@@ -225,6 +244,8 @@
         e = jnp.exp2((st - top) * (SCALE * LOG2E))
         inverse = 1.0 / jnp.sum(e, axis=0, keepdims=True)
         p_t[i, 0:kk] = (e * inverse).astype(BF)
+    m_rings[1][1]()
+    m_near(0)
     for copy in qkv[6:]:
         copy.wait_recv()
     for i in range(4):
@@ -242,54 +263,73 @@
                 push(a_loc.at[a, (s + o) % 4], a_r.at[a, s], a_s.at[at], a_rs.at[at], seq_at(o))
             )
 
-    m_y[2].wait_recv()
-    m_across(1, (y + 3) % 4)
-    m_y[1].wait_recv()
-    m_across(2, (y + 1) % 4)
-    m_y[4].wait_recv()
-    m_y[5].wait_recv()
-    m_across(3, (y + 2) % 4)
-    for copy in m_c:
-        copy.wait_recv()
-
-    x_opposite, x_left, x_right, x_relay, x_result = ring_sum(xp, x_land, head_at, h, x_s, x_r)
-    for n, send in enumerate((x_opposite, x_left, x_right, None)):
+    m_far(0)
+    m_near(1)
+    for copy in m_c[0]:
+        copy.wait_recv()
+
+    x_rings = [
+        ring_sum(
+            lambda j, half, k=k: xp.at[j, 2 * k + half], x_land.at[k], head_at, h, x_s.at[k], x_r.at[k]
+        )
+        for k in range(2)
+    ]
+
+    def x_rows(n, step):
         a = h_order[n]
+        for t in (2 * step, 2 * step + 1):
+            xp[a, t] = nn(af[a], m_all[t]).astype(BF)
+        if n < 3:
+            x_rings[step][n]()
+
+    for n, a in enumerate(h_order):
         for copy in a_cp[3 * n : 3 * n + 3]:
             copy.wait_recv()
         for src in range(4):
             af[a, :, src * HD : src * HD + HD] = a_r[a, src]
-        for t in range(4):
-            there = slice((t % 2) * 512, (t % 2) * 512 + 512)
-            xp[a, t // 2, :, there] = nn(af[a], m_all[t]).astype(BF)
-        if send is not None:
-            send()
-    x_relay()
+        x_rows(n, 0)
+    m_far(1)
+    for copy in m_c[1]:
+        copy.wait_recv()
+    x_rows(0, 1)
+    x_rings[0][3]()
+    for n in (1, 2, 3):
+        x_rows(n, 1)
     for step in range(2):
         pe_w[step] = pe_v[:, step, :].astype(F32)
         ct_w[step] = ct_v[:, step, :].astype(F32)
     for i in range(2):
         at = transposed(af[:, :, i * 256 : i * 256 + 256].reshape(256, 256))
         aft[i] = at.reshape(4, 64, 256)
-    gx_start, gx_relay, gx_cp = ring_gather(
-        lambda j, half: gx_all.at[j, half], head_at, h, gx_s, gx_r
-    )
+    gx_rings = [
+        ring_gather(
+            lambda j, half, k=k: gx_all.at[j, 2 * k + half], head_at, h, gx_s.at[k], gx_r.at[k]
+        )
+        for k in range(2)
+    ]
     for step in range(2):
-        x = x_result(step) + pe_w[step]
+        if step == 0:
+            x_rings[1][3]()
+        x = jnp.concatenate([x_rings[step][4](half) for half in range(2)], axis=1) + pe_w[step]
         r = lax.rsqrt(jnp.mean(x * x, axis=-1, keepdims=True) + 1e-05)
         normed = x * r
         co = ct_w[step]
         gx = r * (co - normed * jnp.mean(co * normed, axis=-1, keepdims=True))
-        gx_all[h, step] = gx.astype(BF)
-        gx_start(step)
+        for half in range(2):
+            gx_all[h, 2 * step + half] = gx[:, half * 512 : half * 512 + 512].astype(BF)
+            gx_rings[step][0](half)
+
+    def gx_wait(*which):
+        for ring_of in gx_rings:
+            for n in which:
+                ring_of[2][n].wait_recv()
 
     ga_cp = []
 
     def grad_rows(n, a):
         ga = jnp.zeros((64, 512), F32)
         for t in range(4):
-            there = slice((t % 2) * 512, (t % 2) * 512 + 512)
-            ga += nt(gx_all[a, t // 2, :, there], m_all[t])
+            ga += nt(gx_all[a, t], m_all[t])
         for src in range(4):
             ga_f[a, src] = ga[:, src * HD : src * HD + HD].astype(BF)
         ga_h[a, s] = ga_f[a, s]
@@ -300,38 +340,48 @@
             )
 
     grad_rows(0, h)
-    gx_relay()
-    gx_cp[2].wait_recv()
+    for ring_of in gx_rings:
+        ring_of[1]()
+    gx_wait(2)
     grad_rows(1, (h + 3) % 4)
-    gx_cp[1].wait_recv()
+    gx_wait(1)
     grad_rows(2, (h + 1) % 4)
-    gx_cp[4].wait_recv()
-    gx_cp[5].wait_recv()
+    gx_wait(4, 5)
     grad_rows(3, (h + 2) % 4)
 
     y_order = [(y + o) % 4 for o in (2, 3, 1, 0)]
 
-    def g_rows(core, index, step):
-        return nn(aft[core, index], gx_all[:, step].reshape(256, 1024))
+    def g_rows(core, index, t):
+        return nn(aft[core, index], gx_all[:, t].reshape(256, 512))
 
     g1 = []
     for n, index in enumerate(y_order):
-        for step in range(2):
-            g_send[index, step] = g_rows(1 - c, index, step).astype(BF)
+        for t in range(4):
+            g_send[index, t] = g_rows(1 - c, index, t).astype(BF)
         g1.append(push(g_send.at[index], g_r1.at[index], g1_s.at[n], g1_r.at[n], core_at))
 
-    g_opposite, g_left, g_right, g_relay, g_result = ring_sum(g2, g_land, y_at, y, g2_s, g2_r)
-    for n, send in enumerate((g_opposite, g_left, g_right, None)):
-        index = y_order[n]
-        own = [g_rows(c, index, step) for step in range(2)]
+    def g_view(j, half, part):
+        return g2.at[j, 2 * half : 2 * half + 2, :, part * 256 : part * 256 + 256]
+
+    g_rings = [
+        ring_sum(
+            lambda j, half, part=part: g_view(j, half, part),
+            g_land.at[part], y_at, y, g2_s.at[part], g2_r.at[part],
+        )
+        for part in range(2)
+    ]
+    for n, index in enumerate(y_order):
+        own = [g_rows(c, index, t) for t in range(4)]
         g1[n].wait_recv()
-        for step in range(2):
-            g2[index, step] = (own[step] + g_r1[index, step].astype(F32)).astype(BF)
-        if send is not None:
-            send()
-
+        for t in range(4):
+            g2[index, t] = (own[t] + g_r1[index, t].astype(F32)).astype(BF)
+        if n == 0:
+            g_rings[0][0]()
+            g_rings[1][0]()
     for copy in ga_cp:
         copy.wait_recv()
+    g_rings[0][1]()
+    g_rings[0][2]()
 
     def backward(i):
         kk = (i + 1) * 256
@@ -367,57 +417,66 @@
         out_own.append(pltpu.make_async_copy(src.at[s], there, loc.at[16 + n]))
         out_own[-1].start()
 
+    g_rings[0][3]()
+    g_rings[1][1]()
+    g_rings[1][2]()
     give(0)
-    g_relay()
+    g_rings[1][3]()
+    g3c = []
+    for part in range(2):
+        for half in range(2):
+            total = g_rings[part][4](half).astype(BF)
+            for t in range(2):
+                g3[part, :, 2 * half + t] = total[t].reshape(2, 32, 256)
+        for o in range(1, 8):
+            oz, os = z_at(o)
+            at = part * 7 + o - 1
+            g3c.append(
+                push(g3.at[part, oz, os], g_r3.at[at], g3_s.at[at], g3_r.at[at], z_device(o))
+            )
+    g4c = []
+    for part in range(2):
+        total = g3[part, zh, s].astype(F32)
+        for o in range(1, 8):
+            g3c[part * 7 + o - 1].wait_recv()
+            total += g_r3[part * 7 + o - 1].astype(F32)
+        grow[part, s, zh] = total.astype(BF)
+        here = grow.at[part, s, zh]
+        for o in range(1, 8):
+            at = part * 7 + o - 1
+            g4c.append(push(here, here, g4_s.at[at], g4_r.at[at], z_device(o)))
     give(1)
-    for step in range(2):
-        total = g_result(step)
-        for t in range(2):
-            there = total[:, t * 512 : t * 512 + 512].astype(BF)
-            g3[:, 2 * step + t] = there.reshape(2, 32, 512)
-    g3c = []
-    for o in range(1, 8):
-        oz, os = z_at(o)
-        g3c.append(
-            push(g3.at[oz, os], g_r3.at[o - 1], g3_s.at[o - 1], g3_r.at[o - 1], z_device(o))
-        )
-    for copy in g3c:
-        copy.wait_recv()
-    total = g3[zh, s].astype(F32)
-    for o in range(1, 8):
-        total += g_r3[o - 1].astype(F32)
-    grow[s, zh] = total.astype(BF)
-    g4c = [
-        push(grow.at[s, zh], grow.at[s, zh], g4_s.at[o - 1], g4_r.at[o - 1], z_device(o))
-        for o in range(1, 8)
-    ]
-    give(2)
-    for copy in g4c:
-        copy.wait_recv()
-
-    for j in range(8):
-        there = slice(j * 64, j * 64 + 64)
-        pair = [grow[2 * step + zh, :, :, there].reshape(64, 64) for step in range(2)]
-        gperm[j] = jnp.concatenate(pair, axis=1)
-    block = c * 4 + y
-    gcol[block] = gperm[g % 8]
-    gcc = [
-        push(
-            gperm.at[(g + o) % 8], gcol.at[block], gc_s.at[o - 1], gc_r.at[o - 1], half_at(o)
-        )
-        for o in range(1, 8)
-    ]
+    mine = [jnp.zeros((64, 512), F32) for _ in range(2)]
+    for part in range(2):
+        for copy in g4c[7 * part : 7 * part + 7]:
+            copy.wait_recv()
+        for j in range(4):
+            there = slice(j * 64, j * 64 + 64)
+            pair = [grow[part, 2 * k + zh, :, :, there].reshape(64, 64) for k in range(2)]
+            gperm[4 * part + j] = jnp.concatenate(pair, axis=1)
+        if part:
+            block = c * 4 + y
+            gcol[block] = gperm[g % 8]
+            gcc = [
+                push(
+                    gperm.at[(g + o) % 8], gcol.at[block], gc_s.at[o - 1], gc_r.at[o - 1], half_at(o)
+                )
+                for o in range(1, 8)
+            ]
+        for t in range(4):
+            rows = grow[part, t].reshape(64, 256)
+            for half in range(2):
+                first = (t % 2) * 512 + part * 256
+                depth = d_v[t // 2, half * 512 : half * 512 + 512, first : first + 256]
+                mine[half] += nt(rows, depth)
     y_cp = []
     for half in range(2):
-        mine = jnp.zeros((64, 512), F32)
-        for t in range(4):
-            depth = d_v[t // 2, half * 512 : half * 512 + 512, (t % 2) * 512 : (t % 2) * 512 + 512]
-            mine += nt(grow[t].reshape(64, 512), depth)
-        dop[half, m_rows(y)] = mine.astype(BF)
+        dop[half, m_rows(y)] = mine[half].astype(BF)
         here = dop.at[half, m_rows(y)]
         for o in ring:
             at = half * 3 + o - 1
             y_cp.append(push(here, here, y_s.at[at], y_r.at[at], y_at(o)))
+    give(2)
 
     c1, dw_c = [], []
 
@@ -465,27 +524,9 @@
         copy.wait_send()
 
 
-def widen(dq, dk, dv, dw, dd, *refs):
-    outs, (narrow, tokens, weight, load, store) = refs[:5], refs[5:]
-    parts = [(src.at[0], dst.at[0], tokens.at[n]) for n, (src, dst) in enumerate(zip((dq, dk, dv), outs))]
-    for n in range(4):
-        rows = slice(n * 128, n * 128 + 128)
-        for half in range(2):
-            at = (rows, slice(half * 512, half * 512 + 512))
-            parts.append((dw.at[at], outs[3].at[at], weight.at[n, half]))
-    held = [narrow.at[n] if n < 3 else narrow.at[n, 0:128] for n in range(11)]
-    loads = [pltpu.make_async_copy(p[0], held[n], load.at[n]) for n, p in enumerate(parts)]
-    stores = [pltpu.make_async_copy(p[2], p[1], store.at[n]) for n, p in enumerate(parts)]
-    stores.append(pltpu.make_async_copy(dd, outs[4], store.at[11]))
-    stores[11].start()
-    for copy in loads:
-        copy.start()
-    for n, part in enumerate(parts):
-        loads[n].wait()
-        part[2][...] = held[n][...].astype(F32)
-        stores[n].start()
-    for copy in stores:
-        copy.wait()
+def widen(*refs):
+    for src, dst in zip(refs[:5], refs[5:]):
+        dst[...] = src[...].astype(F32)
 
 
 def shards(t_query, t_key, t_value, out_proj, depth_in, prev_embed, cotangent):
@@ -507,17 +548,17 @@
             vmem((4, 64, 512)), vmem((3, 64, 512)), vmem((64, 512)), vmem((4, 512, 512)),
             vmem((HD, 1024)), vmem((HD, 1024)), vmem((4, 1024, 256)),
             vmem((4, 4, 64, HD)), vmem((4, 4, 64, HD)), vmem((4, 64, 512)), vmem((2, 4, 64, 256)),
-            vmem((4, 2, 64, 1024)), vmem((6, 64, 1024)), vmem((4, 2, 64, 1024)),
+            vmem((4, 4, 64, 512)), vmem((2, 6, 64, 512)), vmem((4, 4, 64, 512)),
             vmem((4, 4, 64, HD)), vmem((4, 4, 64, HD)),
             vmem((1024, HD), F32), vmem((1024, HD), F32),
             vmem((4, 256, HD)), vmem((4, 256, HD)), vmem((4, 256, HD)),
-            vmem((4, 2, 64, 1024)), vmem((4, 2, 64, 1024)), vmem((4, 2, 64, 1024)),
-            vmem((6, 64, 1024)), vmem((2, 4, 32, 512)), vmem((7, 32, 512)),
-            vmem((4, 2, 32, 512)), vmem((2, 512, 512)), vmem((8, 64, HD)), vmem((8, 64, HD)),
+            vmem((4, 4, 64, 512)), vmem((4, 4, 64, 512)), vmem((4, 4, 64, 512)),
+            vmem((2, 6, 2, 64, 256)), vmem((2, 2, 4, 32, 256)), vmem((14, 32, 256)),
+            vmem((2, 4, 2, 32, 256)), vmem((2, 512, 512)), vmem((8, 64, HD)), vmem((8, 64, HD)),
             vmem((4, HD, 256)), vmem((3, HD, 256)), vmem((HD, 256), F32),
-            dma(19), dma(9), dma(9), dma(4), dma(4), dma(4), dma(4), dma(6), dma(6), dma(4), dma(4),
-            dma(12), dma(12), dma(6), dma(6), dma(6), dma(6), dma(12), dma(12), dma(9), dma(9),
-            dma(4), dma(4), dma(6), dma(6), dma(7), dma(7), dma(7), dma(7), dma(7), dma(7),
+            dma(19), dma(9), dma(9), dma(4), dma(4), dma(4), dma(4), dma(2, 6), dma(2, 6), dma(8), dma(8),
+            dma(12), dma(12), dma(2, 6), dma(2, 6), dma(2, 6), dma(2, 6), dma(12), dma(12), dma(9), dma(9),
+            dma(4), dma(4), dma(2, 6), dma(2, 6), dma(14), dma(14), dma(14), dma(14), dma(7), dma(7),
             dma(3), dma(3), dma(6), dma(6), dma(8), dma(8),
         ],
         compiler_params=pltpu.CompilerParams(
@@ -525,14 +566,16 @@
         ),
     )(t_query, t_key, t_value, out_proj, depth_in, prev_embed, cotangent)
     wide = lambda *shape: jax.ShapeDtypeStruct(shape, F32)
+    tokens = pl.BlockSpec((1, 128, 512), lambda i: (0, i, 0))
+    weight = pl.BlockSpec((256, 1024), lambda i: (i, 0))
+    depth = pl.BlockSpec((64, 256), lambda i: (i, 0))
+    specs = [tokens, tokens, tokens, weight, depth]
     dq, dk, dv, dw, dd = pl.pallas_call(
         widen,
+        grid=(2,),
+        in_specs=specs,
+        out_specs=specs,
         out_shape=(wide(1, 256, 512), wide(1, 256, 512), wide(1, 256, 512), wide(512, 1024), wide(HD, 256)),
-        in_specs=[pl.BlockSpec(memory_space=pl.ANY)] * 5,
-        out_specs=[pl.BlockSpec(memory_space=pl.ANY)] * 5,
-        scratch_shapes=[
-            vmem((11, 256, 512)), vmem((3, 256, 512), F32), vmem((4, 2, 128, 512), F32), dma(11), dma(12),
-        ],
         compiler_params=pltpu.CompilerParams(vmem_limit_bytes=60 * 1024 * 1024),
     )(dq, dk, dv, dw, dd)
     return dq, dk, dv, dw, jnp.transpose(dd.reshape(2, 64, 256), (0, 2, 1))

time: 118 us -> 107 us (0.907)
  Pallas kernels: 117 us -> 107 us
    pallas_call x1, Pallas kernels: 112 us -> 104 us  [shards(): pl.pallas_call(kernel, out_shape=(frames, frames, frames, jax.ShapeDtypeS...]
    pallas_call x1, Pallas kernels: 5.28 us -> 3.15 us  [shards(): pl.pallas_call(widen, grid=(2,), in_specs=specs, out_specs=specs, out_sha...]
where the time goes in v3:
time: 107 us
  Pallas kernels  107 us (100%)
    pallas_call x1, Pallas kernels, shards(): pl.pallas_call(kernel, out_shape=(frames, frames, frames, jax.ShapeDtypeS...  104 us
    pallas_call x1, Pallas kernels, shards(): pl.pallas_call(widen, grid=(2,), in_specs=specs, out_specs=specs, out_sha...  3.15 us

profile of v3, /device:TPU:1, one launch (start us, length us, event | category | flops | bytes accessed | tf_op | source)
XLA Modules:
  0.0 107.4 jit_solution(12030209342741259350)
XLA Ops:
  0.6 103.6 %shard_map.110 = (bf16[1,256,512]{2,1,0:T(8,128)(2,1)}, bf16[1,256,512]{2,1,0:T(8,128)(2,1)}, bf16[1,256,512]{2,1,0:T(8,128)(2,1)}, bf16[512,1024]{1,0:T(8,128)(2,1)}, f32[128,256]{1,0:T(8,128)}) custom-call(bf16[1,256,512]{2,1,0:T(8,128)(2,1)} %q.1, bf16[1,256,512]{2,1,0:T(8,128)(2,1)} %k.1, bf16[1,256,512]{2,1,0:T(8,128)(2,1)} %v.1, bf16[512,1024]{1,0:T(8,128)(2,1)} %wo.1, ...), custom_call_target="tpu_custom_call" | custom-call | tf_op jit(solution)/shard_map/pallas_call | solution.py:536
  104.2 3.2 %shard_map.111 = (f32[1,256,512]{2,1,0:T(8,128)}, f32[1,256,512]{2,1,0:T(8,128)}, f32[1,256,512]{2,1,0:T(8,128)}, f32[512,1024]{1,0:T(8,128)}, f32[128,256]{1,0:T(8,128)}) custom-call(bf16[1,256,512]{2,1,0:T(8,128)(2,1)} %get-tuple-element.15.refs_0_, bf16[1,256,512]{2,1,0:T(8,128)(2,1)} %get-tuple-element.16.refs_1_, ...), custom_call_target="tpu_custom_call" | custom-call | tf_op jit(solution)/shard_map/pallas_call | solution.py:573

commit v4 on v3

--- a/solution.py
+++ b/solution.py
@@ -171,7 +171,7 @@
     qkv = []
 
     def spread(n, src, dst):
-        for o in ring:
+        for o in (2, 1, 3):
             at = n * 3 + o - 1
             there = src.at[0, :, cols((s + o) % 4)]
             qkv.append(push(there, dst.at[s], qkv_s.at[at], qkv_r.at[at], seq_at(o)))
@@ -257,7 +257,7 @@
     a_cp = []
     for n, a in enumerate(h_order):
         a_r[a, s] = a_loc[a, s]
-        for o in ring:
+        for o in (2, 1, 3):
             at = n * 3 + o - 1
             a_cp.append(
                 push(a_loc.at[a, (s + o) % 4], a_r.at[a, s], a_s.at[at], a_rs.at[at], seq_at(o))
@@ -347,7 +347,6 @@
     gx_wait(1)
     grad_rows(2, (h + 1) % 4)
     gx_wait(4, 5)
-    grad_rows(3, (h + 2) % 4)
 
     y_order = [(y + o) % 4 for o in (2, 3, 1, 0)]
 
@@ -359,6 +358,7 @@
         for t in range(4):
             g_send[index, t] = g_rows(1 - c, index, t).astype(BF)
         g1.append(push(g_send.at[index], g_r1.at[index], g1_s.at[n], g1_r.at[n], core_at))
+    grad_rows(3, (h + 2) % 4)
 
     def g_view(j, half, part):
         return g2.at[j, 2 * half : 2 * half + 2, :, part * 256 : part * 256 + 256]
@@ -411,16 +411,16 @@
     def give(n):
         src, dst = outs[n]
         there = dst.at[0, :, cols(s)]
-        for o in ring:
+        for o in (2, 1, 3):
             at = n * 3 + o - 1
             out_cp.append(push(src.at[(s + o) % 4], there, o_s.at[at], o_r.at[at], seq_at(o)))
         out_own.append(pltpu.make_async_copy(src.at[s], there, loc.at[16 + n]))
         out_own[-1].start()
 
+    give(0)
     g_rings[0][3]()
     g_rings[1][1]()
     g_rings[1][2]()
-    give(0)
     g_rings[1][3]()
     g3c = []
     for part in range(2):
@@ -445,7 +445,6 @@
         for o in range(1, 8):
             at = part * 7 + o - 1
             g4c.append(push(here, here, g4_s.at[at], g4_r.at[at], z_device(o)))
-    give(1)
     mine = [jnp.zeros((64, 512), F32) for _ in range(2)]
     for part in range(2):
         for copy in g4c[7 * part : 7 * part + 7]:
@@ -476,6 +475,7 @@
         for o in ring:
             at = half * 3 + o - 1
             y_cp.append(push(here, here, y_s.at[at], y_r.at[at], y_at(o)))
+    give(1)
     give(2)
 
     c1, dw_c = [], []

time: 107 us -> 105 us (0.981)
  Pallas kernels: 107 us -> 104 us
    pallas_call x1, Pallas kernels: 104 us -> 101 us  [shards(): pl.pallas_call(kernel, out_shape=(frames, frames, frames, jax.ShapeDtypeS...]
where the time goes in v4:
time: 105 us
  Pallas kernels  104 us (99%)
    pallas_call x1, Pallas kernels, shards(): pl.pallas_call(kernel, out_shape=(frames, frames, frames, jax.ShapeDtypeS...  101 us
    pallas_call x1, Pallas kernels, shards(): pl.pallas_call(widen, grid=(2,), in_specs=specs, out_specs=specs, out_sha...  3.15 us

profile of v4, /device:TPU:1, one launch (start us, length us, event | category | flops | bytes accessed | tf_op | source)
XLA Modules:
  0.0 105.0 jit_solution(12470814283298324616)
XLA Ops:
  0.6 101.2 %shard_map.110 = (bf16[1,256,512]{2,1,0:T(8,128)(2,1)}, bf16[1,256,512]{2,1,0:T(8,128)(2,1)}, bf16[1,256,512]{2,1,0:T(8,128)(2,1)}, bf16[512,1024]{1,0:T(8,128)(2,1)}, f32[128,256]{1,0:T(8,128)}) custom-call(bf16[1,256,512]{2,1,0:T(8,128)(2,1)} %q.1, bf16[1,256,512]{2,1,0:T(8,128)(2,1)} %k.1, bf16[1,256,512]{2,1,0:T(8,128)(2,1)} %v.1, bf16[512,1024]{1,0:T(8,128)(2,1)} %wo.1, ...), custom_call_target="tpu_custom_call" | custom-call | tf_op jit(solution)/shard_map/pallas_call | solution.py:536
  101.9 3.2 %shard_map.111 = (f32[1,256,512]{2,1,0:T(8,128)}, f32[1,256,512]{2,1,0:T(8,128)}, f32[1,256,512]{2,1,0:T(8,128)}, f32[512,1024]{1,0:T(8,128)}, f32[128,256]{1,0:T(8,128)}) custom-call(bf16[1,256,512]{2,1,0:T(8,128)(2,1)} %get-tuple-element.15.refs_0_, bf16[1,256,512]{2,1,0:T(8,128)(2,1)} %get-tuple-element.16.refs_1_, ...), custom_call_target="tpu_custom_call" | custom-call | tf_op jit(solution)/shard_map/pallas_call | solution.py:573

commit v5 on v4

--- a/solution.py
+++ b/solution.py
@@ -333,7 +333,7 @@
         for src in range(4):
             ga_f[a, src] = ga[:, src * HD : src * HD + HD].astype(BF)
         ga_h[a, s] = ga_f[a, s]
-        for o in ring:
+        for o in (2, 1, 3):
             at = n * 3 + o - 1
             ga_cp.append(
                 push(ga_f.at[a, (s + o) % 4], ga_h.at[a, s], ga_s.at[at], ga_r.at[at], seq_at(o))
@@ -422,17 +422,18 @@
     g_rings[1][1]()
     g_rings[1][2]()
     g_rings[1][3]()
-    g3c = []
+    z_order = (4, 3, 5, 2, 6, 1, 7)
+    g3c = {}
     for part in range(2):
         for half in range(2):
             total = g_rings[part][4](half).astype(BF)
             for t in range(2):
                 g3[part, :, 2 * half + t] = total[t].reshape(2, 32, 256)
-        for o in range(1, 8):
+        for o in z_order:
             oz, os = z_at(o)
             at = part * 7 + o - 1
-            g3c.append(
-                push(g3.at[part, oz, os], g_r3.at[at], g3_s.at[at], g3_r.at[at], z_device(o))
+            g3c[at] = push(
+                g3.at[part, oz, os], g_r3.at[at], g3_s.at[at], g3_r.at[at], z_device(o)
             )
     g4c = []
     for part in range(2):
@@ -442,7 +443,7 @@
             total += g_r3[part * 7 + o - 1].astype(F32)
         grow[part, s, zh] = total.astype(BF)
         here = grow.at[part, s, zh]
-        for o in range(1, 8):
+        for o in z_order:
             at = part * 7 + o - 1
             g4c.append(push(here, here, g4_s.at[at], g4_r.at[at], z_device(o)))
     mine = [jnp.zeros((64, 512), F32) for _ in range(2)]

time: 105 us -> 106 us (level)
  no operation moved by 1% of the time
where the time goes in v5:
time: 106 us
  Pallas kernels  105 us (99%)
    pallas_call x1, Pallas kernels, shards(): pl.pallas_call(kernel, out_shape=(frames, frames, frames, jax.ShapeDtypeS...  102 us
    pallas_call x1, Pallas kernels, shards(): pl.pallas_call(widen, grid=(2,), in_specs=specs, out_specs=specs, out_sha...  3.15 us

profile of v5, /device:TPU:1, one launch (start us, length us, event | category | flops | bytes accessed | tf_op | source)
XLA Modules:
  0.0 105.9 jit_solution(16781662960868784544)
XLA Ops:
  0.6 102.1 %shard_map.110 = (bf16[1,256,512]{2,1,0:T(8,128)(2,1)}, bf16[1,256,512]{2,1,0:T(8,128)(2,1)}, bf16[1,256,512]{2,1,0:T(8,128)(2,1)}, bf16[512,1024]{1,0:T(8,128)(2,1)}, f32[128,256]{1,0:T(8,128)}) custom-call(bf16[1,256,512]{2,1,0:T(8,128)(2,1)} %q.1, bf16[1,256,512]{2,1,0:T(8,128)(2,1)} %k.1, bf16[1,256,512]{2,1,0:T(8,128)(2,1)} %v.1, bf16[512,1024]{1,0:T(8,128)(2,1)} %wo.1, ...), custom_call_target="tpu_custom_call" | custom-call | tf_op jit(solution)/shard_map/pallas_call | solution.py:537
  102.8 3.2 %shard_map.111 = (f32[1,256,512]{2,1,0:T(8,128)}, f32[1,256,512]{2,1,0:T(8,128)}, f32[1,256,512]{2,1,0:T(8,128)}, f32[512,1024]{1,0:T(8,128)}, f32[128,256]{1,0:T(8,128)}) custom-call(bf16[1,256,512]{2,1,0:T(8,128)(2,1)} %get-tuple-element.15.refs_0_, bf16[1,256,512]{2,1,0:T(8,128)(2,1)} %get-tuple-element.16.refs_1_, ...), custom_call_target="tpu_custom_call" | custom-call | tf_op jit(solution)/shard_map/pallas_call | solution.py:574
